TPU v7x, 256 devices: a whole 4x4x8 slice. The times are simulated.
256 devices in a mesh: freq: 4 (over z_lo), slab: 16 (over y, x), xy: 4 (over z_hi, core).
Axes of the slice: x: 4, y: 4, z: 8 (z_hi: 2, z_lo: 4; z = z_hi * 4 + z_lo), core: 2. Of those that a mesh axis runs over, the one named last changes fastest.
Arguments:
- previous_field: float32 [2, 64, 128, 512], P(None, 'xy', 'slab', 'freq'), may hold values from -6 to 6
- current_field: float32 [2, 64, 128, 512], P(None, 'xy', 'slab', 'freq'), may hold values from -6 to 6
- courant: float32 [64, 128, 512], P('xy', 'slab', 'freq'), may hold values from 0.05 to 0.3
- wavelet: float32 [16], replicated, may hold values from -16 to 16
- traces: float32 [16, 256], replicated, may hold values from -12 to 12
- source_cell: int32 [1], replicated, may hold values from 0 to 4194303
- receiver_cells: int32 [256], replicated, may hold values from 0 to 4194303
- frequency_list: int32 [32], replicated, may hold values from 1 to 255
- lag_list: int32 [17], replicated, may hold values from -16 to 16, as said below
- spectra: float32 [2, 32, 2, 4, 16, 128, 512], P(None, 'freq', None, 'xy', 'slab'), may hold values from -24 to 24
Outputs:
- image: bfloat16 [17, 4, 16, 128, 512], P(None, 'xy', 'slab', 'freq')
Inputs may be any that keep to these rules, and one draw needn't show every extreme that they name: `lag_list`: the list holds both -16 and 16. `receiver_cells`: receivers may share a cell.
All inputs are finite; a program needn't handle non-finite values.
Results may differ from a plain program's by a relative error of at most 0.02.
Values may be sent and summed in bfloat16 or wider, within the bound.
A program may use at most 128 MiB of HBM per device.

v0:
```python
import math

import jax
import jax.numpy as jnp
from jax import lax
from jax.sharding import PartitionSpec as P

STEPS = 16
NTOT = 2048
LAGMAX = 16


def extended(x, sides, width):
    for axis, dim in sides:
        size, length = (lax.axis_size(axis), x.shape[dim])
        up = [(i, (i + 1) % size) for i in range(size - 1)]
        down = [(j, i) for i, j in up]
        last = lax.slice_in_dim(x, length - width, length, axis=dim)
        initial = lax.slice_in_dim(x, 0, width, axis=dim)
        before = lax.ppermute(last, axis, up)
        after = lax.ppermute(initial, axis, down)
        x = jnp.concatenate([before, x, after], axis=dim)
    return x


def dft_table(frequency_list):
    moments = jnp.arange(STEPS, dtype=jnp.int32) + (NTOT - STEPS)
    phase_index = moments[:, None] * frequency_list[None, :] % NTOT
    phase_angle = phase_index.astype(jnp.float32) * (2.0 * math.pi / NTOT)
    return jnp.stack([jnp.cos(phase_angle), -jnp.sin(phase_angle)], axis=-1).astype(jnp.bfloat16)


def transform(planes, dft_rows):
    flat_snap = planes.reshape(planes.shape[0], planes.shape[1], -1)
    return jnp.einsum("tkp,tfc->fkpc", dft_rows, flat_snap, preferred_element_type=jnp.float32)


def body(
    previous_field,
    current_field,
    courant,
    wavelet,
    traces,
    source_cell,
    receiver_cells,
    frequency_list,
    lag_list,
    spectra,
):
    fields, depth_rows, row_count, col_count = current_field.shape
    slab_count = lax.axis_size("slab")
    freq_count = lax.axis_size("freq")
    total_rows = row_count * slab_count
    total_cols = col_count * freq_count
    depth_start = lax.axis_index("xy") * depth_rows
    row_start = lax.axis_index("slab") * row_count
    column_start = lax.axis_index("freq") * col_count
    local_cells = depth_rows * row_count * col_count

    def locate(cell_ids):
        plane_size = total_rows * total_cols
        depth_index = cell_ids // plane_size - depth_start
        row_index = cell_ids // total_cols % total_rows - row_start
        column = cell_ids % total_cols - column_start
        inside = (
            (depth_index >= 0)
            & (depth_index < depth_rows)
            & (row_index >= 0)
            & (row_index < row_count)
            & (column >= 0)
            & (column < col_count)
        )
        cell_place = jnp.where(
            inside, (depth_index * row_count + row_index) * col_count + column, 0
        )
        return (cell_place, inside.astype(jnp.float32))

    source_place, source_inside = locate(source_cell)
    receiver_place, receiver_inside = locate(receiver_cells)

    def advance(state, inputs):
        previous, current = state
        pulse_value, trace_row = inputs
        padded = extended(
            current.astype(jnp.bfloat16), (("freq", 3), ("slab", 2), ("xy", 1)), 1
        ).astype(current.dtype)
        beside = padded[:, 2:, 1:-1, 1:-1] + padded[:, :-2, 1:-1, 1:-1]
        beside = beside + padded[:, 1:-1, 2:, 1:-1] + padded[:, 1:-1, :-2, 1:-1]
        beside = beside + padded[:, 1:-1, 1:-1, 2:] + padded[:, 1:-1, 1:-1, :-2]
        injection = jnp.zeros((fields, local_cells), jnp.float32)
        injection = injection.at[0, source_place].add(pulse_value * source_inside)
        injection = injection.at[1, receiver_place].add(trace_row * receiver_inside)
        following = (
            2.0 * current
            - previous
            + courant * (beside - 6.0 * current)
            + injection.reshape(current.shape)
        )
        return ((current, following), following.astype(jnp.bfloat16))

    end_state, snapshots = lax.scan(advance, (previous_field, current_field), (wavelet, traces))
    dft_rows = dft_table(frequency_list)
    own_count = spectra.shape[1]
    own_rows = lax.dynamic_slice_in_dim(dft_rows, lax.axis_index("freq") * own_count, own_count, 1)
    wide_snap = lax.all_gather(snapshots, "freq", axis=4, tiled=True)
    planes = lax.all_to_all(wide_snap, "slab", split_axis=2, concat_axis=3, tiled=True)
    window_part = transform(planes, own_rows)
    new_spectra = spectra + window_part.reshape(spectra.shape)
    term_count = own_count * 2
    plane_shape = new_spectra.shape[4:]
    widths = ((0, 0), (0, 0), (0, 0), (LAGMAX, LAGMAX))
    padded_source = jnp.pad(new_spectra[0].reshape((term_count,) + plane_shape), widths)
    padded_receiver = jnp.pad(new_spectra[1].reshape((term_count,) + plane_shape), widths)
    weight = 1.0 / (STEPS * dft_rows.shape[1])

    def one_lag(offset_value):
        early_terms = lax.dynamic_slice_in_dim(padded_source, LAGMAX - offset_value, total_cols, 3)
        late_terms = lax.dynamic_slice_in_dim(padded_receiver, LAGMAX + offset_value, total_cols, 3)
        return jnp.sum(early_terms * late_terms, axis=0) * weight

    partial_image = lax.map(one_lag, lag_list)
    summed_image = lax.psum_scatter(
        partial_image.astype(jnp.bfloat16), "freq", scatter_dimension=2, tiled=True
    ).astype(jnp.float32)
    return summed_image.astype(jnp.bfloat16).reshape(
        (lag_list.shape[0], 1) + summed_image.shape[1:]
    )


def solution(mesh):
    placed = (
        P(None, "xy", "slab", "freq"),
        P(None, "xy", "slab", "freq"),
        P("xy", "slab", "freq"),
        P(),
        P(),
        P(),
        P(),
        P(),
        P(),
        P(None, "freq", None, "xy", "slab", None, None),
    )
    return jax.shard_map(
        body,
        mesh=mesh,
        in_specs=placed,
        out_specs=P(None, "xy", "slab", "freq", None),
        check_vma=False,
    )
```

profile of v0, /device:TPU:1, one launch (start us, length us, event | category | flops | bytes accessed | tf_op | source)
XLA Modules:
  0.0 1128.2 jit_solution(17601191863693484519)
XLA Ops:
  11.9 682.4 %while.32 = (s32[]{:T(128)}, f32[2,16,8,128]{3,2,1,0:T(8,128)S(1)}, f32[2,16,8,128]{3,2,1,0:T(8,128)S(1)}, bf16[16,2,16,8,128]{4,3,1,0,2:T(8,128)(2,1)}, f32[16,...) while((s32[]{:T(128)}, f32[2,16,8,128]{3,2,1,0:T(8,128)S(1)}, ...), condition=%wide.region_3.4_spmd, body=%wide.region_1.3_spmd.sunk | while | flops 1218436 | bytes 3271654 | solution.py:101
  26.3 6.4 collective-permute-start.4
  32.7 7.0 collective-permute-start.5
  43.1 12.6 %scatter_fusion = f32[2,16384]{1,0:T(2,128)S(1)} fusion(f32[2,16384]{1,0:T(2,128)S(1)} %scatter-add.20, s32[256]{0:T(256)S(1)} %bitcast.67, f32[256]{0:T(256)S(1)} %mul.209), kind=kCustom, calls=%fused_computation.clone.1 | custom fusion | flops 256 | bytes 5120 | tf_op jit(solution)/shard_map/while/body/eval_jaxpr/scatter-add | solution.py:92
  73.4 7.5 collective-permute-start.5
  84.4 12.6 %scatter_fusion = f32[2,16384]{1,0:T(2,128)S(1)} fusion(f32[2,16384]{1,0:T(2,128)S(1)} %scatter-add.20, s32[256]{0:T(256)S(1)} %bitcast.67, f32[256]{0:T(256)S(1)} %mul.209), kind=kCustom, calls=%fused_computation.clone.1 | custom fusion | flops 256 | bytes 5120 | tf_op jit(solution)/shard_map/while/body/eval_jaxpr/scatter-add | solution.py:92
  114.1 7.5 collective-permute-start.5
  125.1 12.6 %scatter_fusion = f32[2,16384]{1,0:T(2,128)S(1)} fusion(f32[2,16384]{1,0:T(2,128)S(1)} %scatter-add.20, s32[256]{0:T(256)S(1)} %bitcast.67, f32[256]{0:T(256)S(1)} %mul.209), kind=kCustom, calls=%fused_computation.clone.1 | custom fusion | flops 256 | bytes 5120 | tf_op jit(solution)/shard_map/while/body/eval_jaxpr/scatter-add | solution.py:92
  154.9 7.5 collective-permute-start.5
  165.8 12.6 %scatter_fusion = f32[2,16384]{1,0:T(2,128)S(1)} fusion(f32[2,16384]{1,0:T(2,128)S(1)} %scatter-add.20, s32[256]{0:T(256)S(1)} %bitcast.67, f32[256]{0:T(256)S(1)} %mul.209), kind=kCustom, calls=%fused_computation.clone.1 | custom fusion | flops 256 | bytes 5120 | tf_op jit(solution)/shard_map/while/body/eval_jaxpr/scatter-add | solution.py:92
  188.3 6.9 collective-permute-start.3
  198.2 7.5 collective-permute-start.5
  209.2 12.6 %scatter_fusion = f32[2,16384]{1,0:T(2,128)S(1)} fusion(f32[2,16384]{1,0:T(2,128)S(1)} %scatter-add.20, s32[256]{0:T(256)S(1)} %bitcast.67, f32[256]{0:T(256)S(1)} %mul.209), kind=kCustom, calls=%fused_computation.clone.1 | custom fusion | flops 256 | bytes 5120 | tf_op jit(solution)/shard_map/while/body/eval_jaxpr/scatter-add | solution.py:92
  231.6 6.4 collective-permute-start.3
  241.0 7.5 collective-permute-start.5
  252.0 12.6 %scatter_fusion = f32[2,16384]{1,0:T(2,128)S(1)} fusion(f32[2,16384]{1,0:T(2,128)S(1)} %scatter-add.20, s32[256]{0:T(256)S(1)} %bitcast.67, f32[256]{0:T(256)S(1)} %mul.209), kind=kCustom, calls=%fused_computation.clone.1 | custom fusion | flops 256 | bytes 5120 | tf_op jit(solution)/shard_map/while/body/eval_jaxpr/scatter-add | solution.py:92
  274.5 6.4 collective-permute-start.3
  283.9 7.5 collective-permute-start.5
  294.9 12.6 %scatter_fusion = f32[2,16384]{1,0:T(2,128)S(1)} fusion(f32[2,16384]{1,0:T(2,128)S(1)} %scatter-add.20, s32[256]{0:T(256)S(1)} %bitcast.67, f32[256]{0:T(256)S(1)} %mul.209), kind=kCustom, calls=%fused_computation.clone.1 | custom fusion | flops 256 | bytes 5120 | tf_op jit(solution)/shard_map/while/body/eval_jaxpr/scatter-add | solution.py:92
  317.3 6.4 collective-permute-start.3
  326.8 7.5 collective-permute-start.5
  337.7 12.6 %scatter_fusion = f32[2,16384]{1,0:T(2,128)S(1)} fusion(f32[2,16384]{1,0:T(2,128)S(1)} %scatter-add.20, s32[256]{0:T(256)S(1)} %bitcast.67, f32[256]{0:T(256)S(1)} %mul.209), kind=kCustom, calls=%fused_computation.clone.1 | custom fusion | flops 256 | bytes 5120 | tf_op jit(solution)/shard_map/while/body/eval_jaxpr/scatter-add | solution.py:92
  360.2 6.4 collective-permute-start.3
  369.6 7.5 collective-permute-start.5
  380.6 12.6 %scatter_fusion = f32[2,16384]{1,0:T(2,128)S(1)} fusion(f32[2,16384]{1,0:T(2,128)S(1)} %scatter-add.20, s32[256]{0:T(256)S(1)} %bitcast.67, f32[256]{0:T(256)S(1)} %mul.209), kind=kCustom, calls=%fused_computation.clone.1 | custom fusion | flops 256 | bytes 5120 | tf_op jit(solution)/shard_map/while/body/eval_jaxpr/scatter-add | solution.py:92
  403.0 6.4 collective-permute-start.3
  412.4 7.5 collective-permute-start.5
  423.4 12.6 %scatter_fusion = f32[2,16384]{1,0:T(2,128)S(1)} fusion(f32[2,16384]{1,0:T(2,128)S(1)} %scatter-add.20, s32[256]{0:T(256)S(1)} %bitcast.67, f32[256]{0:T(256)S(1)} %mul.209), kind=kCustom, calls=%fused_computation.clone.1 | custom fusion | flops 256 | bytes 5120 | tf_op jit(solution)/shard_map/while/body/eval_jaxpr/scatter-add | solution.py:92
  445.8 6.4 collective-permute-start.3
  455.3 7.5 collective-permute-start.5
  466.3 12.6 %scatter_fusion = f32[2,16384]{1,0:T(2,128)S(1)} fusion(f32[2,16384]{1,0:T(2,128)S(1)} %scatter-add.20, s32[256]{0:T(256)S(1)} %bitcast.67, f32[256]{0:T(256)S(1)} %mul.209), kind=kCustom, calls=%fused_computation.clone.1 | custom fusion | flops 256 | bytes 5120 | tf_op jit(solution)/shard_map/while/body/eval_jaxpr/scatter-add | solution.py:92
  488.7 6.4 collective-permute-start.3
  498.1 7.5 collective-permute-start.5
  509.1 12.6 %scatter_fusion = f32[2,16384]{1,0:T(2,128)S(1)} fusion(f32[2,16384]{1,0:T(2,128)S(1)} %scatter-add.20, s32[256]{0:T(256)S(1)} %bitcast.67, f32[256]{0:T(256)S(1)} %mul.209), kind=kCustom, calls=%fused_computation.clone.1 | custom fusion | flops 256 | bytes 5120 | tf_op jit(solution)/shard_map/while/body/eval_jaxpr/scatter-add | solution.py:92
  531.5 6.4 collective-permute-start.3
  540.9 7.5 collective-permute-start.5
  551.9 12.6 %scatter_fusion = f32[2,16384]{1,0:T(2,128)S(1)} fusion(f32[2,16384]{1,0:T(2,128)S(1)} %scatter-add.20, s32[256]{0:T(256)S(1)} %bitcast.67, f32[256]{0:T(256)S(1)} %mul.209), kind=kCustom, calls=%fused_computation.clone.1 | custom fusion | flops 256 | bytes 5120 | tf_op jit(solution)/shard_map/while/body/eval_jaxpr/scatter-add | solution.py:92
  574.3 6.4 collective-permute-start.3
  583.8 7.5 collective-permute-start.5
  594.8 12.6 %scatter_fusion = f32[2,16384]{1,0:T(2,128)S(1)} fusion(f32[2,16384]{1,0:T(2,128)S(1)} %scatter-add.20, s32[256]{0:T(256)S(1)} %bitcast.67, f32[256]{0:T(256)S(1)} %mul.209), kind=kCustom, calls=%fused_computation.clone.1 | custom fusion | flops 256 | bytes 5120 | tf_op jit(solution)/shard_map/while/body/eval_jaxpr/scatter-add | solution.py:92
  617.2 6.4 collective-permute-start.3
  626.6 7.5 collective-permute-start.5
  637.6 12.6 %scatter_fusion = f32[2,16384]{1,0:T(2,128)S(1)} fusion(f32[2,16384]{1,0:T(2,128)S(1)} %scatter-add.20, s32[256]{0:T(256)S(1)} %bitcast.67, f32[256]{0:T(256)S(1)} %mul.209), kind=kCustom, calls=%fused_computation.clone.1 | custom fusion | flops 256 | bytes 5120 | tf_op jit(solution)/shard_map/while/body/eval_jaxpr/scatter-add | solution.py:92
  660.0 6.4 collective-permute-start.3
  669.4 7.5 collective-permute-start.5
  680.4 12.6 %scatter_fusion = f32[2,16384]{1,0:T(2,128)S(1)} fusion(f32[2,16384]{1,0:T(2,128)S(1)} %scatter-add.20, s32[256]{0:T(256)S(1)} %bitcast.67, f32[256]{0:T(256)S(1)} %mul.209), kind=kCustom, calls=%fused_computation.clone.1 | custom fusion | flops 256 | bytes 5120 | tf_op jit(solution)/shard_map/while/body/eval_jaxpr/scatter-add | solution.py:92
  694.3 94.7 %all-gather.2.cloned.1.call-done = bf16[16,2,16,8,512]{4,3,1,0,2:T(8,128)(2,1)} async-done(((bf16[16,2,16,8,128]{4,3,1,0,2:T(8,128)(2,1)}), bf16[16,2,16,8,512]{4,3,1,0,2:T(8,128)(2,1)}) %all-gather.2.cloned.1.call-update) | async-done | bytes 4194320 | tf_op jit(solution)/shard_map/all_gather | solution.py:105
  795.1 62.2 %all-to-all-done = bf16[16,2,16,8,512]{4,3,1,0,2:T(8,128)(2,1)} async-done(((bf16[16,2,16,8,512]{4,3,1,0,2:T(8,128)(2,1)}), bf16[16,2,16,8,512]{4,3,1,0,2:T(8,128)(2,1)}, u32[]{:S(2)}, u32[]{:S(2)}) %all-to-all-start) | async-done | bytes 4194336 | tf_op jit(solution)/shard_map/all_to_all | solution.py:106
  867.7 6.8 fusion.4
  874.5 14.4 %copy_add_fusion = f32[2,8,2,1,1,128,512]{6,5,4,3,2,1,0:T(8,128)} fusion(f32[2,8,2,1,1,128,512]{6,5,4,3,2,1,0:T(8,128)} %param.25, f32[2,8,2,1,1,128,512]{6,1,5,2,0,4,3:T(8,128)} %bitcast.69), kind=kLoop, calls=%fused_computation.28 | loop fusion | flops 2097152 | bytes 25165824 | tf_op jit(solution)/shard_map/add | solution.py:108
  900.9 171.7 %while.33 = (s32[]{:T(128)}, bf16[17,1,128,512]{3,2,1,0:T(8,128)(2,1)}, s32[17]{0:T(128)S(1)}, f32[16,1,128,544]{3,2,1,0:T(8,128)}, f32[16,1,128,544]{3,2,1,0:T(...) while((s32[]{:T(128)}, bf16[17,1,128,512]{3,2,1,0:T(8,128)(2,1)}, s32[17]{0:T(128)S(1)}, ...), condition=%wide.region_6.7_spmd, body=%wide.region_4.6_spmd.sunk | while | flops 2097162 | bytes 9175757 | solution.py:121
  904.0 6.3 multiply_reduce_fusion.2
  914.1 6.3 multiply_reduce_fusion.2
  924.2 6.3 multiply_reduce_fusion.2
  934.3 6.3 multiply_reduce_fusion.2
  944.4 6.3 multiply_reduce_fusion.2
  954.5 6.3 multiply_reduce_fusion.2
  964.6 6.3 multiply_reduce_fusion.2
  974.7 6.3 multiply_reduce_fusion.2
  984.8 6.3 multiply_reduce_fusion.2
  994.9 6.3 multiply_reduce_fusion.2
  1005.0 6.3 multiply_reduce_fusion.2
  1015.1 6.3 multiply_reduce_fusion.2
  1072.6 48.8 %reduce-scatter.2.cloned.1.call-done = bf16[17,1,32,512]{3,2,0,1:T(8,128)(2,1)} async-done(((bf16[17,1,128,512]{3,2,0,1:T(8,128)(2,1)}), bf16[17,1,32,512]{3,2,0,1:T(8,128)(2,1)}) %reduce-scatter.2.cloned.1.call-update) | async-done | bytes 557072 | tf_op jit(solution)/shard_map/reduce_scatter | solution.py:122
  (497 shorter events, 339.3 us)
Async XLA Ops:
  6.5 782.5 %all-gather.2.cloned.1.call-start = ((), (), s32[]{:S(2)}) async-start(), calls=%async_computation.2 | async-start | bytes 5242880 | tf_op jit(solution)/shard_map/all_gather | solution.py:105
  12.0 6.3 collective-permute-start
  13.3 6.3 collective-permute-start.1
  26.3 29.4 %collective-permute-start.4 = (bf16[2,1,10,130]{3,2,1,0:T(8,128)(2,1)S(1)}, bf16[2,1,10,130]{3,2,1,0:T(8,128)(2,1)S(1)}, u32[]{:S(2)}, u32[]{:S(2)}) collective-permute-start(bf16[2,1,10,130]{3,2,1,0:T(8,128)(2,1)S(1)} %get-tuple-element.479), channel_id=1, source_target_pairs={{1,0},{2,1},{3,2},{5,4},{6,5},{7,6},{9,8},{10,9},{11,10},{13,12},{... | collective-permute-start | bytes 15608 | tf_op jit(solution)/shard_map/while/body/eval_jaxpr/ppermute | solution.py:21
  32.7 23.0 %collective-permute-start.5 = (bf16[2,1,10,130]{3,2,1,0:T(8,128)(2,1)S(1)}, bf16[2,1,10,130]{3,2,1,0:T(8,128)(2,1)S(1)}, u32[]{:S(2)}, u32[]{:S(2)}) collective-permute-start(bf16[2,1,10,130]{3,2,1,0:T(8,128)(2,1)S(1)} %get-tuple-element.480), channel_id=1, source_target_pairs={{0,1},{1,2},{2,3},{4,5},{5,6},{6,7},{8,9},{9,10},{10,11},{12,13},{... | collective-permute-start | bytes 15608 | tf_op jit(solution)/shard_map/while/body/eval_jaxpr/ppermute | solution.py:20
  57.1 5.9 collective-permute-start
  58.4 5.9 collective-permute-start.1
  64.5 5.9 collective-permute-start.2
  71.5 25.5 %collective-permute-start.4 = (bf16[2,1,10,130]{3,2,1,0:T(8,128)(2,1)S(1)}, bf16[2,1,10,130]{3,2,1,0:T(8,128)(2,1)S(1)}, u32[]{:S(2)}, u32[]{:S(2)}) collective-permute-start(bf16[2,1,10,130]{3,2,1,0:T(8,128)(2,1)S(1)} %get-tuple-element.479), channel_id=1, source_target_pairs={{1,0},{2,1},{3,2},{5,4},{6,5},{7,6},{9,8},{10,9},{11,10},{13,12},{... | collective-permute-start | bytes 15608 | tf_op jit(solution)/shard_map/while/body/eval_jaxpr/ppermute | solution.py:21
  73.4 23.6 %collective-permute-start.5 = (bf16[2,1,10,130]{3,2,1,0:T(8,128)(2,1)S(1)}, bf16[2,1,10,130]{3,2,1,0:T(8,128)(2,1)S(1)}, u32[]{:S(2)}, u32[]{:S(2)}) collective-permute-start(bf16[2,1,10,130]{3,2,1,0:T(8,128)(2,1)S(1)} %get-tuple-element.480), channel_id=1, source_target_pairs={{0,1},{1,2},{2,3},{4,5},{5,6},{6,7},{8,9},{9,10},{10,11},{12,13},{... | collective-permute-start | bytes 15608 | tf_op jit(solution)/shard_map/while/body/eval_jaxpr/ppermute | solution.py:20
  112.2 25.5 %collective-permute-start.4 = (bf16[2,1,10,130]{3,2,1,0:T(8,128)(2,1)S(1)}, bf16[2,1,10,130]{3,2,1,0:T(8,128)(2,1)S(1)}, u32[]{:S(2)}, u32[]{:S(2)}) collective-permute-start(bf16[2,1,10,130]{3,2,1,0:T(8,128)(2,1)S(1)} %get-tuple-element.479), channel_id=1, source_target_pairs={{1,0},{2,1},{3,2},{5,4},{6,5},{7,6},{9,8},{10,9},{11,10},{13,12},{... | collective-permute-start | bytes 15608 | tf_op jit(solution)/shard_map/while/body/eval_jaxpr/ppermute | solution.py:21
  114.1 23.6 %collective-permute-start.5 = (bf16[2,1,10,130]{3,2,1,0:T(8,128)(2,1)S(1)}, bf16[2,1,10,130]{3,2,1,0:T(8,128)(2,1)S(1)}, u32[]{:S(2)}, u32[]{:S(2)}) collective-permute-start(bf16[2,1,10,130]{3,2,1,0:T(8,128)(2,1)S(1)} %get-tuple-element.480), channel_id=1, source_target_pairs={{0,1},{1,2},{2,3},{4,5},{5,6},{6,7},{8,9},{9,10},{10,11},{12,13},{... | collective-permute-start | bytes 15608 | tf_op jit(solution)/shard_map/while/body/eval_jaxpr/ppermute | solution.py:20
  152.9 25.5 %collective-permute-start.4 = (bf16[2,1,10,130]{3,2,1,0:T(8,128)(2,1)S(1)}, bf16[2,1,10,130]{3,2,1,0:T(8,128)(2,1)S(1)}, u32[]{:S(2)}, u32[]{:S(2)}) collective-permute-start(bf16[2,1,10,130]{3,2,1,0:T(8,128)(2,1)S(1)} %get-tuple-element.479), channel_id=1, source_target_pairs={{1,0},{2,1},{3,2},{5,4},{6,5},{7,6},{9,8},{10,9},{11,10},{13,12},{... | collective-permute-start | bytes 15608 | tf_op jit(solution)/shard_map/while/body/eval_jaxpr/ppermute | solution.py:21
  154.9 23.6 %collective-permute-start.5 = (bf16[2,1,10,130]{3,2,1,0:T(8,128)(2,1)S(1)}, bf16[2,1,10,130]{3,2,1,0:T(8,128)(2,1)S(1)}, u32[]{:S(2)}, u32[]{:S(2)}) collective-permute-start(bf16[2,1,10,130]{3,2,1,0:T(8,128)(2,1)S(1)} %get-tuple-element.480), channel_id=1, source_target_pairs={{0,1},{1,2},{2,3},{4,5},{5,6},{6,7},{8,9},{9,10},{10,11},{12,13},{... | collective-permute-start | bytes 15608 | tf_op jit(solution)/shard_map/while/body/eval_jaxpr/ppermute | solution.py:20
  187.0 8.2 collective-permute-start.2
  188.3 7.9 collective-permute-start.3
  196.3 25.5 %collective-permute-start.4 = (bf16[2,1,10,130]{3,2,1,0:T(8,128)(2,1)S(1)}, bf16[2,1,10,130]{3,2,1,0:T(8,128)(2,1)S(1)}, u32[]{:S(2)}, u32[]{:S(2)}) collective-permute-start(bf16[2,1,10,130]{3,2,1,0:T(8,128)(2,1)S(1)} %get-tuple-element.479), channel_id=1, source_target_pairs={{1,0},{2,1},{3,2},{5,4},{6,5},{7,6},{9,8},{10,9},{11,10},{13,12},{... | collective-permute-start | bytes 15608 | tf_op jit(solution)/shard_map/while/body/eval_jaxpr/ppermute | solution.py:21
  198.2 23.6 %collective-permute-start.5 = (bf16[2,1,10,130]{3,2,1,0:T(8,128)(2,1)S(1)}, bf16[2,1,10,130]{3,2,1,0:T(8,128)(2,1)S(1)}, u32[]{:S(2)}, u32[]{:S(2)}) collective-permute-start(bf16[2,1,10,130]{3,2,1,0:T(8,128)(2,1)S(1)} %get-tuple-element.480), channel_id=1, source_target_pairs={{0,1},{1,2},{2,3},{4,5},{5,6},{6,7},{8,9},{9,10},{10,11},{12,13},{... | collective-permute-start | bytes 15608 | tf_op jit(solution)/shard_map/while/body/eval_jaxpr/ppermute | solution.py:20
  230.3 7.7 collective-permute-start.2
  231.6 7.4 collective-permute-start.3
  239.1 25.5 %collective-permute-start.4 = (bf16[2,1,10,130]{3,2,1,0:T(8,128)(2,1)S(1)}, bf16[2,1,10,130]{3,2,1,0:T(8,128)(2,1)S(1)}, u32[]{:S(2)}, u32[]{:S(2)}) collective-permute-start(bf16[2,1,10,130]{3,2,1,0:T(8,128)(2,1)S(1)} %get-tuple-element.479), channel_id=1, source_target_pairs={{1,0},{2,1},{3,2},{5,4},{6,5},{7,6},{9,8},{10,9},{11,10},{13,12},{... | collective-permute-start | bytes 15608 | tf_op jit(solution)/shard_map/while/body/eval_jaxpr/ppermute | solution.py:21
  241.0 23.6 %collective-permute-start.5 = (bf16[2,1,10,130]{3,2,1,0:T(8,128)(2,1)S(1)}, bf16[2,1,10,130]{3,2,1,0:T(8,128)(2,1)S(1)}, u32[]{:S(2)}, u32[]{:S(2)}) collective-permute-start(bf16[2,1,10,130]{3,2,1,0:T(8,128)(2,1)S(1)} %get-tuple-element.480), channel_id=1, source_target_pairs={{0,1},{1,2},{2,3},{4,5},{5,6},{6,7},{8,9},{9,10},{10,11},{12,13},{... | collective-permute-start | bytes 15608 | tf_op jit(solution)/shard_map/while/body/eval_jaxpr/ppermute | solution.py:20
  273.2 7.7 collective-permute-start.2
  274.5 7.4 collective-permute-start.3
  282.0 25.5 %collective-permute-start.4 = (bf16[2,1,10,130]{3,2,1,0:T(8,128)(2,1)S(1)}, bf16[2,1,10,130]{3,2,1,0:T(8,128)(2,1)S(1)}, u32[]{:S(2)}, u32[]{:S(2)}) collective-permute-start(bf16[2,1,10,130]{3,2,1,0:T(8,128)(2,1)S(1)} %get-tuple-element.479), channel_id=1, source_target_pairs={{1,0},{2,1},{3,2},{5,4},{6,5},{7,6},{9,8},{10,9},{11,10},{13,12},{... | collective-permute-start | bytes 15608 | tf_op jit(solution)/shard_map/while/body/eval_jaxpr/ppermute | solution.py:21
  283.9 23.6 %collective-permute-start.5 = (bf16[2,1,10,130]{3,2,1,0:T(8,128)(2,1)S(1)}, bf16[2,1,10,130]{3,2,1,0:T(8,128)(2,1)S(1)}, u32[]{:S(2)}, u32[]{:S(2)}) collective-permute-start(bf16[2,1,10,130]{3,2,1,0:T(8,128)(2,1)S(1)} %get-tuple-element.480), channel_id=1, source_target_pairs={{0,1},{1,2},{2,3},{4,5},{5,6},{6,7},{8,9},{9,10},{10,11},{12,13},{... | collective-permute-start | bytes 15608 | tf_op jit(solution)/shard_map/while/body/eval_jaxpr/ppermute | solution.py:20
  316.0 7.7 collective-permute-start.2
  317.3 7.4 collective-permute-start.3
  324.8 25.5 %collective-permute-start.4 = (bf16[2,1,10,130]{3,2,1,0:T(8,128)(2,1)S(1)}, bf16[2,1,10,130]{3,2,1,0:T(8,128)(2,1)S(1)}, u32[]{:S(2)}, u32[]{:S(2)}) collective-permute-start(bf16[2,1,10,130]{3,2,1,0:T(8,128)(2,1)S(1)} %get-tuple-element.479), channel_id=1, source_target_pairs={{1,0},{2,1},{3,2},{5,4},{6,5},{7,6},{9,8},{10,9},{11,10},{13,12},{... | collective-permute-start | bytes 15608 | tf_op jit(solution)/shard_map/while/body/eval_jaxpr/ppermute | solution.py:21
  326.8 23.6 %collective-permute-start.5 = (bf16[2,1,10,130]{3,2,1,0:T(8,128)(2,1)S(1)}, bf16[2,1,10,130]{3,2,1,0:T(8,128)(2,1)S(1)}, u32[]{:S(2)}, u32[]{:S(2)}) collective-permute-start(bf16[2,1,10,130]{3,2,1,0:T(8,128)(2,1)S(1)} %get-tuple-element.480), channel_id=1, source_target_pairs={{0,1},{1,2},{2,3},{4,5},{5,6},{6,7},{8,9},{9,10},{10,11},{12,13},{... | collective-permute-start | bytes 15608 | tf_op jit(solution)/shard_map/while/body/eval_jaxpr/ppermute | solution.py:20
  358.9 7.7 collective-permute-start.2
  360.2 7.4 collective-permute-start.3
  367.7 25.5 %collective-permute-start.4 = (bf16[2,1,10,130]{3,2,1,0:T(8,128)(2,1)S(1)}, bf16[2,1,10,130]{3,2,1,0:T(8,128)(2,1)S(1)}, u32[]{:S(2)}, u32[]{:S(2)}) collective-permute-start(bf16[2,1,10,130]{3,2,1,0:T(8,128)(2,1)S(1)} %get-tuple-element.479), channel_id=1, source_target_pairs={{1,0},{2,1},{3,2},{5,4},{6,5},{7,6},{9,8},{10,9},{11,10},{13,12},{... | collective-permute-start | bytes 15608 | tf_op jit(solution)/shard_map/while/body/eval_jaxpr/ppermute | solution.py:21
  369.6 23.6 %collective-permute-start.5 = (bf16[2,1,10,130]{3,2,1,0:T(8,128)(2,1)S(1)}, bf16[2,1,10,130]{3,2,1,0:T(8,128)(2,1)S(1)}, u32[]{:S(2)}, u32[]{:S(2)}) collective-permute-start(bf16[2,1,10,130]{3,2,1,0:T(8,128)(2,1)S(1)} %get-tuple-element.480), channel_id=1, source_target_pairs={{0,1},{1,2},{2,3},{4,5},{5,6},{6,7},{8,9},{9,10},{10,11},{12,13},{... | collective-permute-start | bytes 15608 | tf_op jit(solution)/shard_map/while/body/eval_jaxpr/ppermute | solution.py:20
  401.7 7.7 collective-permute-start.2
  403.0 7.4 collective-permute-start.3
  410.5 25.5 %collective-permute-start.4 = (bf16[2,1,10,130]{3,2,1,0:T(8,128)(2,1)S(1)}, bf16[2,1,10,130]{3,2,1,0:T(8,128)(2,1)S(1)}, u32[]{:S(2)}, u32[]{:S(2)}) collective-permute-start(bf16[2,1,10,130]{3,2,1,0:T(8,128)(2,1)S(1)} %get-tuple-element.479), channel_id=1, source_target_pairs={{1,0},{2,1},{3,2},{5,4},{6,5},{7,6},{9,8},{10,9},{11,10},{13,12},{... | collective-permute-start | bytes 15608 | tf_op jit(solution)/shard_map/while/body/eval_jaxpr/ppermute | solution.py:21
  412.4 23.6 %collective-permute-start.5 = (bf16[2,1,10,130]{3,2,1,0:T(8,128)(2,1)S(1)}, bf16[2,1,10,130]{3,2,1,0:T(8,128)(2,1)S(1)}, u32[]{:S(2)}, u32[]{:S(2)}) collective-permute-start(bf16[2,1,10,130]{3,2,1,0:T(8,128)(2,1)S(1)} %get-tuple-element.480), channel_id=1, source_target_pairs={{0,1},{1,2},{2,3},{4,5},{5,6},{6,7},{8,9},{9,10},{10,11},{12,13},{... | collective-permute-start | bytes 15608 | tf_op jit(solution)/shard_map/while/body/eval_jaxpr/ppermute | solution.py:20
  444.5 7.7 collective-permute-start.2
  445.8 7.4 collective-permute-start.3
  453.3 25.5 %collective-permute-start.4 = (bf16[2,1,10,130]{3,2,1,0:T(8,128)(2,1)S(1)}, bf16[2,1,10,130]{3,2,1,0:T(8,128)(2,1)S(1)}, u32[]{:S(2)}, u32[]{:S(2)}) collective-permute-start(bf16[2,1,10,130]{3,2,1,0:T(8,128)(2,1)S(1)} %get-tuple-element.479), channel_id=1, source_target_pairs={{1,0},{2,1},{3,2},{5,4},{6,5},{7,6},{9,8},{10,9},{11,10},{13,12},{... | collective-permute-start | bytes 15608 | tf_op jit(solution)/shard_map/while/body/eval_jaxpr/ppermute | solution.py:21
  455.3 23.6 %collective-permute-start.5 = (bf16[2,1,10,130]{3,2,1,0:T(8,128)(2,1)S(1)}, bf16[2,1,10,130]{3,2,1,0:T(8,128)(2,1)S(1)}, u32[]{:S(2)}, u32[]{:S(2)}) collective-permute-start(bf16[2,1,10,130]{3,2,1,0:T(8,128)(2,1)S(1)} %get-tuple-element.480), channel_id=1, source_target_pairs={{0,1},{1,2},{2,3},{4,5},{5,6},{6,7},{8,9},{9,10},{10,11},{12,13},{... | collective-permute-start | bytes 15608 | tf_op jit(solution)/shard_map/while/body/eval_jaxpr/ppermute | solution.py:20
  487.4 7.7 collective-permute-start.2
  488.7 7.4 collective-permute-start.3
  496.2 25.5 %collective-permute-start.4 = (bf16[2,1,10,130]{3,2,1,0:T(8,128)(2,1)S(1)}, bf16[2,1,10,130]{3,2,1,0:T(8,128)(2,1)S(1)}, u32[]{:S(2)}, u32[]{:S(2)}) collective-permute-start(bf16[2,1,10,130]{3,2,1,0:T(8,128)(2,1)S(1)} %get-tuple-element.479), channel_id=1, source_target_pairs={{1,0},{2,1},{3,2},{5,4},{6,5},{7,6},{9,8},{10,9},{11,10},{13,12},{... | collective-permute-start | bytes 15608 | tf_op jit(solution)/shard_map/while/body/eval_jaxpr/ppermute | solution.py:21
  498.1 23.6 %collective-permute-start.5 = (bf16[2,1,10,130]{3,2,1,0:T(8,128)(2,1)S(1)}, bf16[2,1,10,130]{3,2,1,0:T(8,128)(2,1)S(1)}, u32[]{:S(2)}, u32[]{:S(2)}) collective-permute-start(bf16[2,1,10,130]{3,2,1,0:T(8,128)(2,1)S(1)} %get-tuple-element.480), channel_id=1, source_target_pairs={{0,1},{1,2},{2,3},{4,5},{5,6},{6,7},{8,9},{9,10},{10,11},{12,13},{... | collective-permute-start | bytes 15608 | tf_op jit(solution)/shard_map/while/body/eval_jaxpr/ppermute | solution.py:20
  530.2 7.7 collective-permute-start.2
  531.5 7.4 collective-permute-start.3
  539.0 25.5 %collective-permute-start.4 = (bf16[2,1,10,130]{3,2,1,0:T(8,128)(2,1)S(1)}, bf16[2,1,10,130]{3,2,1,0:T(8,128)(2,1)S(1)}, u32[]{:S(2)}, u32[]{:S(2)}) collective-permute-start(bf16[2,1,10,130]{3,2,1,0:T(8,128)(2,1)S(1)} %get-tuple-element.479), channel_id=1, source_target_pairs={{1,0},{2,1},{3,2},{5,4},{6,5},{7,6},{9,8},{10,9},{11,10},{13,12},{... | collective-permute-start | bytes 15608 | tf_op jit(solution)/shard_map/while/body/eval_jaxpr/ppermute | solution.py:21
  540.9 23.6 %collective-permute-start.5 = (bf16[2,1,10,130]{3,2,1,0:T(8,128)(2,1)S(1)}, bf16[2,1,10,130]{3,2,1,0:T(8,128)(2,1)S(1)}, u32[]{:S(2)}, u32[]{:S(2)}) collective-permute-start(bf16[2,1,10,130]{3,2,1,0:T(8,128)(2,1)S(1)} %get-tuple-element.480), channel_id=1, source_target_pairs={{0,1},{1,2},{2,3},{4,5},{5,6},{6,7},{8,9},{9,10},{10,11},{12,13},{... | collective-permute-start | bytes 15608 | tf_op jit(solution)/shard_map/while/body/eval_jaxpr/ppermute | solution.py:20
  573.0 7.7 collective-permute-start.2
  574.3 7.4 collective-permute-start.3
  581.8 25.5 %collective-permute-start.4 = (bf16[2,1,10,130]{3,2,1,0:T(8,128)(2,1)S(1)}, bf16[2,1,10,130]{3,2,1,0:T(8,128)(2,1)S(1)}, u32[]{:S(2)}, u32[]{:S(2)}) collective-permute-start(bf16[2,1,10,130]{3,2,1,0:T(8,128)(2,1)S(1)} %get-tuple-element.479), channel_id=1, source_target_pairs={{1,0},{2,1},{3,2},{5,4},{6,5},{7,6},{9,8},{10,9},{11,10},{13,12},{... | collective-permute-start | bytes 15608 | tf_op jit(solution)/shard_map/while/body/eval_jaxpr/ppermute | solution.py:21
  583.8 23.6 %collective-permute-start.5 = (bf16[2,1,10,130]{3,2,1,0:T(8,128)(2,1)S(1)}, bf16[2,1,10,130]{3,2,1,0:T(8,128)(2,1)S(1)}, u32[]{:S(2)}, u32[]{:S(2)}) collective-permute-start(bf16[2,1,10,130]{3,2,1,0:T(8,128)(2,1)S(1)} %get-tuple-element.480), channel_id=1, source_target_pairs={{0,1},{1,2},{2,3},{4,5},{5,6},{6,7},{8,9},{9,10},{10,11},{12,13},{... | collective-permute-start | bytes 15608 | tf_op jit(solution)/shard_map/while/body/eval_jaxpr/ppermute | solution.py:20
  615.9 7.7 collective-permute-start.2
  617.2 7.4 collective-permute-start.3
  624.7 25.5 %collective-permute-start.4 = (bf16[2,1,10,130]{3,2,1,0:T(8,128)(2,1)S(1)}, bf16[2,1,10,130]{3,2,1,0:T(8,128)(2,1)S(1)}, u32[]{:S(2)}, u32[]{:S(2)}) collective-permute-start(bf16[2,1,10,130]{3,2,1,0:T(8,128)(2,1)S(1)} %get-tuple-element.479), channel_id=1, source_target_pairs={{1,0},{2,1},{3,2},{5,4},{6,5},{7,6},{9,8},{10,9},{11,10},{13,12},{... | collective-permute-start | bytes 15608 | tf_op jit(solution)/shard_map/while/body/eval_jaxpr/ppermute | solution.py:21
  626.6 23.6 %collective-permute-start.5 = (bf16[2,1,10,130]{3,2,1,0:T(8,128)(2,1)S(1)}, bf16[2,1,10,130]{3,2,1,0:T(8,128)(2,1)S(1)}, u32[]{:S(2)}, u32[]{:S(2)}) collective-permute-start(bf16[2,1,10,130]{3,2,1,0:T(8,128)(2,1)S(1)} %get-tuple-element.480), channel_id=1, source_target_pairs={{0,1},{1,2},{2,3},{4,5},{5,6},{6,7},{8,9},{9,10},{10,11},{12,13},{... | collective-permute-start | bytes 15608 | tf_op jit(solution)/shard_map/while/body/eval_jaxpr/ppermute | solution.py:20
  658.7 7.7 collective-permute-start.2
  660.0 7.4 collective-permute-start.3
  667.5 25.5 %collective-permute-start.4 = (bf16[2,1,10,130]{3,2,1,0:T(8,128)(2,1)S(1)}, bf16[2,1,10,130]{3,2,1,0:T(8,128)(2,1)S(1)}, u32[]{:S(2)}, u32[]{:S(2)}) collective-permute-start(bf16[2,1,10,130]{3,2,1,0:T(8,128)(2,1)S(1)} %get-tuple-element.479), channel_id=1, source_target_pairs={{1,0},{2,1},{3,2},{5,4},{6,5},{7,6},{9,8},{10,9},{11,10},{13,12},{... | collective-permute-start | bytes 15608 | tf_op jit(solution)/shard_map/while/body/eval_jaxpr/ppermute | solution.py:21
  669.4 23.6 %collective-permute-start.5 = (bf16[2,1,10,130]{3,2,1,0:T(8,128)(2,1)S(1)}, bf16[2,1,10,130]{3,2,1,0:T(8,128)(2,1)S(1)}, u32[]{:S(2)}, u32[]{:S(2)}) collective-permute-start(bf16[2,1,10,130]{3,2,1,0:T(8,128)(2,1)S(1)} %get-tuple-element.480), channel_id=1, source_target_pairs={{0,1},{1,2},{2,3},{4,5},{5,6},{6,7},{8,9},{9,10},{10,11},{12,13},{... | collective-permute-start | bytes 15608 | tf_op jit(solution)/shard_map/while/body/eval_jaxpr/ppermute | solution.py:20
  789.0 68.4 %all-to-all-start = ((bf16[16,2,16,8,512]{4,3,1,0,2:T(8,128)(2,1)}), bf16[16,2,16,8,512]{4,3,1,0,2:T(8,128)(2,1)}, u32[]{:S(2)}, u32[]{:S(2)}) async-start(bf16[16,2,16,8,512]{4,3,1,0,2:T(8,128)(2,1)} %all-gather.2.cloned.1.call-done), calls=%async_computation | async-start | bytes 8388608 | tf_op jit(solution)/shard_map/all_to_all | solution.py:106
  794.7 326.7 %reduce-scatter.2.cloned.1.call-start = ((), (), s32[]{:S(2)}) async-start(), calls=%async_computation.3 | async-start | bytes 2785280 | tf_op jit(solution)/shard_map/reduce_scatter | solution.py:122
  (53 other events, 966.8 us)
Sparse Core Ops, SparseCore 0:
  694.4 94.5 all-gather.1
  1072.7 48.6 reduce-scatter.1
where the time goes:
time: 1130 us
  starting transfers between devices  367 us (32%)
  other arithmetic  351 us (31%)
  waiting for transfers between devices  242 us (21%)
  local copies, waits for them, and re-layouts  80.2 us (7%)
  loops' own time  66.8 us (6%)
  between operations  14.3 us (1%)
    ppermute x48, starting transfers between devices, extended(): before = lax.ppermute(last, axis, up)  285 us
    scatter-add x16, other arithmetic, advance(): injection = injection.at[1, receiver_place].add(trace_row * receiver_inside)  202 us
    reduce_sum x17, other arithmetic, one_lag(): return jnp.sum(early_terms * late_terms, axis=0) * weight  107 us
    all_gather x1, waiting for transfers between devices, body(): wide_snap = lax.all_gather(snapshots, 'freq', axis=4, tiled=True)  94.7 us
    ppermute x48, starting transfers between devices, extended(): after = lax.ppermute(initial, axis, down)  76.6 us
    all_to_all x1, waiting for transfers between devices, body(): lax.all_to_all(wide_snap, 'slab', split_axis=2, concat_axis=3, tiled=True)  62.2 us
    reduce_scatter x1, waiting for transfers between devices, body(): lax.psum_scatter(partial_image.astype(jnp.bfloat16), 'freq', scatter_dime...  48.8 us
    another operation x1, loops' own time, body(): partial_image = lax.map(one_lag, lag_list)  42.8 us
  transfers between devices with their start and end apart: 99, of which 35 were waited for; matrix products, arithmetic and copies ran while one was open for 21% of the time, Pallas kernels for 0%

commit v1 on v0

v1 whole, which is shorter than its diff:
```python
import functools
import math

import jax
import jax.numpy as jnp
from jax import lax
from jax.experimental import pallas as pl
from jax.experimental.pallas import tpu as pltpu
from jax.sharding import PartitionSpec as P

STEPS = 16
NTOT = 2048
LAGMAX = 16
NF, NS, NB = 4, 16, 4
ROWS, COLS = 32, 512
TERMS = 16
NY = NF * ROWS
F32, BF16 = jnp.float32, jnp.bfloat16
MESH = pl.DeviceIdType.MESH


def dft_table(frequency_list):
    moments = jnp.arange(STEPS, dtype=jnp.int32) + (NTOT - STEPS)
    phase_index = moments[:, None] * frequency_list[None, :] % NTOT
    phase_angle = phase_index.astype(F32) * (2.0 * math.pi / NTOT)
    return jnp.stack([jnp.cos(phase_angle), -jnp.sin(phase_angle)], axis=-1).astype(BF16)


def window_kernel(
    prev_ref, cur_ref, cour_ref, wav_ref, traces_ref, src_ref, rec_ref, spec_ref,
    planes, fresh,
    raw, outgoing, pieces_out, pieces_in, field, cour, inj, lo, hi, yout, yin,
    raw_sem, spec_send, spec_recv, piece_send, piece_recv,
    zsend, zrecv, ysend, yrecv,
):
    f, j, b = lax.axis_index("freq"), lax.axis_index("slab"), lax.axis_index("xy")
    z = b * NS + j
    has_lo, has_hi = z > 0, z < NB * NS - 1
    has_top, has_bottom = f > 0, f < NF - 1

    def plane_at(depth):
        return {"freq": f, "slab": depth % NS, "xy": depth // NS}

    def group_at(other):
        return {"freq": other, "slab": j, "xy": b}

    peers = (lax.rem(f + 2, NF), NF - 1 - f, f + 1 - 2 * lax.rem(f, 2))
    chunk = (f,) + peers

    def raw_copy(o, w):
        return pltpu.make_async_copy(
            spec_ref.at[w, :, pl.ds(chunk[o] * ROWS, ROWS), :], raw.at[o, w], raw_sem.at[o, w]
        )

    for o in (1, 2, 3, 0):
        for w in range(2):
            raw_copy(o, w).start()

    barrier = pltpu.get_barrier_semaphore()
    target_f = j // 4
    mine = target_f == f

    for p in peers:
        pl.semaphore_signal(barrier, 1, device_id=group_at(p), device_id_type=MESH)

    @pl.when(has_lo)
    def _():
        pl.semaphore_signal(barrier, 1, device_id=plane_at(z - 1), device_id_type=MESH)

    @pl.when(has_hi)
    def _():
        pl.semaphore_signal(barrier, 1, device_id=plane_at(z + 1), device_id_type=MESH)

    def greet(i, carry):
        f0, j0 = i // 4, 4 * f + i % 4

        @pl.when(jnp.logical_not((f0 == f) & (j0 == j)))
        def _():
            pl.semaphore_signal(
                barrier, 1, device_id={"freq": f0, "slab": j0, "xy": b}, device_id_type=MESH
            )

        return carry

    lax.fori_loop(0, 16, greet, 0)

    def stack(i, carry):
        for w in range(2):
            pieces_out[i, w] = prev_ref[w, i]
            pieces_out[i, 2 + w] = cur_ref[w, i]
        pieces_out[i, 4] = cour_ref[i]
        return carry

    lax.fori_loop(0, NS, stack, 0)

    expected = len(peers) + NS + has_lo.astype(jnp.int32) + has_hi.astype(jnp.int32)
    pl.semaphore_wait(barrier, expected - mine.astype(jnp.int32))

    place = f * 4 + j % 4

    def piece_copy(i):
        return pltpu.make_async_remote_copy(
            src_ref=pieces_out.at[i],
            dst_ref=pieces_in.at[place],
            send_sem=piece_send.at[i],
            recv_sem=piece_recv.at[place],
            device_id={"freq": target_f, "slab": i, "xy": b},
            device_id_type=MESH,
        )

    def is_self(i):
        return mine & (i == j)

    def send_piece(i, carry):
        @pl.when(jnp.logical_not(is_self(i)))
        def _():
            piece_copy(i).start()

        return carry

    lax.fori_loop(0, NS, send_piece, 0)

    @pl.when(mine)
    def _():
        pieces_in[place] = pieces_out[j]

    def spec_copy(o, w):
        return pltpu.make_async_remote_copy(
            src_ref=outgoing.at[o - 1, w],
            dst_ref=fresh.at[f, w],
            send_sem=spec_send.at[o - 1, w],
            recv_sem=spec_recv.at[f, w],
            device_id=group_at(chunk[o]),
            device_id_type=MESH,
        )

    for o in (1, 2, 3):
        for w in range(2):
            raw_copy(o, w).wait()

            def cast(i, carry, o=o, w=w):
                outgoing[o - 1, w, i] = raw[o, w, i].astype(BF16)
                return carry

            lax.fori_loop(0, TERMS, cast, 0)
            spec_copy(o, w).start()

    cell = rec_ref[...]
    depth, row, col = cell >> 16, (cell >> 9) & (NY - 1), cell & (COLS - 1)
    row = jnp.where(depth == z, row - f * ROWS, -1)
    at_row = lax.broadcasted_iota(jnp.int32, (ROWS, cell.shape[1]), 0) == row
    at_col = (lax.broadcasted_iota(jnp.int32, (COLS, cell.shape[1]), 0) == col).astype(F32).astype(BF16)

    def inject(t, carry):
        values = jnp.where(at_row, traces_ref[pl.ds(t, 1), :], 0.0)
        first = values.astype(BF16)
        rest = values - first.astype(F32)
        second = rest.astype(BF16)
        third = (rest - second.astype(F32)).astype(BF16)
        parts = lax.dot_general(
            jnp.concatenate([first, second, third], axis=0), at_col,
            (((1,), (1,)), ((), ())), preferred_element_type=F32,
        )
        inj[t] = parts[:ROWS] + parts[ROWS : 2 * ROWS] + parts[2 * ROWS :]
        return carry

    lax.fori_loop(0, STEPS, inject, 0)

    row_id = lax.broadcasted_iota(jnp.int32, (ROWS, COLS), 0)
    col_id = lax.broadcasted_iota(jnp.int32, (ROWS, COLS), 1)

    for i in range(16):
        f0, jj = i // 4, i % 4

        @pl.when(jnp.logical_not((f == f0) & (j == 4 * f + jj)))
        def _(i=i):
            pltpu.make_async_remote_copy(
                src_ref=pieces_out.at[0], dst_ref=pieces_in.at[i],
                send_sem=piece_send.at[0], recv_sem=piece_recv.at[i],
                device_id=group_at(f), device_id_type=MESH,
            ).wait_recv()

        rows, cols = pl.ds(8 * jj, 8), pl.ds(128 * f0, 128)
        for w in range(2):
            field[1, w, rows, cols] = pieces_in[i, w]
            field[0, w, rows, cols] = pieces_in[i, 2 + w]
        cour[rows, cols] = pieces_in[i, 4]

    def z_copy(s, up):
        return pltpu.make_async_remote_copy(
            src_ref=planes.at[s],
            dst_ref=(lo if up else hi).at[s],
            send_sem=zsend.at[s, int(up)],
            recv_sem=zrecv.at[s, int(up)],
            device_id=plane_at(z + 1 if up else z - 1),
            device_id_type=MESH,
        )

    def y_copy(s, down):
        return pltpu.make_async_remote_copy(
            src_ref=yout.at[s, int(down)],
            dst_ref=yin.at[s, int(down)],
            send_sem=ysend.at[s, int(down)],
            recv_sem=yrecv.at[s, int(down)],
            device_id=group_at(f + 1 if down else f - 1),
            device_id_type=MESH,
        )

    def publish(s, values):
        for w in range(2):
            planes[s, w] = values[w].astype(BF16)

    def send(s, values):
        for w in range(2):
            for i in range(4):
                cols = slice(128 * i, 128 * (i + 1))
                yout[s, 0, pl.ds(4 * w + i, 1), :] = values[w][0:1, cols]
                yout[s, 1, pl.ds(4 * w + i, 1), :] = values[w][ROWS - 1 : ROWS, cols]

        @pl.when(has_hi)
        def _():
            z_copy(s, True).start()

        @pl.when(has_lo)
        def _():
            z_copy(s, False).start()

        @pl.when(has_bottom)
        def _():
            y_copy(s, True).start()

        @pl.when(has_top)
        def _():
            y_copy(s, False).start()

    first = [field[0, w] for w in range(2)]
    publish(0, first)
    send(0, first)

    source = src_ref[0]
    source_row = jnp.where((source >> 16) == z, ((source >> 9) & (NY - 1)) - f * ROWS, -1)
    at_source = (row_id == source_row) & (col_id == (source & (COLS - 1)))

    def arrivals(s, present, copy, there):
        @pl.when(present)
        def _():
            copy.wait_recv()

        @pl.when(jnp.logical_not(present))
        def _():
            there[s] = jnp.zeros(there.shape[1:], there.dtype)

    def advance(t, carry):
        now, other = t % 2, (t + 1) % 2
        arrivals(t, has_lo, z_copy(t, True), lo)
        arrivals(t, has_hi, z_copy(t, False), hi)
        arrivals(t, has_top, y_copy(t, True), yin.at[:, 1])
        arrivals(t, has_bottom, y_copy(t, False), yin.at[:, 0])
        values = []
        for w in range(2):
            u = field[now, w]
            top = jnp.concatenate([yin[t, 1, pl.ds(4 * w + i, 1), :] for i in range(4)], axis=1)
            bottom = jnp.concatenate([yin[t, 0, pl.ds(4 * w + i, 1), :] for i in range(4)], axis=1)
            beside = lo[t, w].astype(F32) + hi[t, w].astype(F32)
            beside += jnp.where(row_id == 0, top, pltpu.roll(u, 1, 0))
            beside += jnp.where(row_id == ROWS - 1, bottom, pltpu.roll(u, ROWS - 1, 0))
            beside += jnp.where(col_id == 0, 0.0, pltpu.roll(u, 1, 1))
            beside += jnp.where(col_id == COLS - 1, 0.0, pltpu.roll(u, COLS - 1, 1))
            injection = inj[t] if w == 1 else jnp.where(at_source, wav_ref[t], 0.0)
            following = 2.0 * u - field[other, w] + cour[...] * (beside - 6.0 * u) + injection
            field[other, w] = following
            values.append(following)
        publish(t + 1, values)

        @pl.when(t < STEPS - 1)
        def _():
            send(t + 1, values)

        return carry

    lax.fori_loop(0, STEPS, advance, 0)

    for w in range(2):
        raw_copy(0, w).wait()

        def cast_own(i, carry, w=w):
            fresh[f, w, i] = raw[0, w, i].astype(BF16)
            return carry

        lax.fori_loop(0, TERMS, cast_own, 0)

    def sent(s, carry):
        @pl.when(has_hi)
        def _():
            z_copy(s, True).wait_send()

        @pl.when(has_lo)
        def _():
            z_copy(s, False).wait_send()

        @pl.when(has_bottom)
        def _():
            y_copy(s, True).wait_send()

        @pl.when(has_top)
        def _():
            y_copy(s, False).wait_send()

        @pl.when(jnp.logical_not(is_self(s)))
        def _():
            piece_copy(s).wait_send()

        return carry

    lax.fori_loop(0, STEPS, sent, 0)

    for o in (1, 2, 3):
        for w in range(2):
            spec_copy(o, w).wait_send()
            pltpu.make_async_remote_copy(
                src_ref=outgoing.at[o - 1, w], dst_ref=fresh.at[chunk[o], w],
                send_sem=spec_send.at[o - 1, w], recv_sem=spec_recv.at[chunk[o], w],
                device_id=group_at(chunk[o]), device_id_type=MESH,
            ).wait_recv()


def window(previous_field, current_field, courant, wavelet, traces, source_cell, receiver_cells, spectra):
    vmem = pl.BlockSpec(memory_space=pltpu.VMEM)
    smem = pl.BlockSpec(memory_space=pltpu.SMEM)
    dma = pltpu.SemaphoreType.DMA
    plane = (2, ROWS, COLS)
    return pl.pallas_call(
        window_kernel,
        out_shape=(
            jax.ShapeDtypeStruct((STEPS + 1,) + plane, BF16),
            jax.ShapeDtypeStruct((NF, 2, TERMS, ROWS, COLS), BF16),
        ),
        in_specs=[vmem, vmem, vmem, smem, vmem, smem, vmem, pl.BlockSpec(memory_space=pl.ANY)],
        out_specs=(vmem, vmem),
        scratch_shapes=[
            pltpu.VMEM((NF, 2, TERMS, ROWS, COLS), F32),
            pltpu.VMEM((NF - 1, 2, TERMS, ROWS, COLS), BF16),
            pltpu.VMEM((NS, 5, 8, 128), F32),
            pltpu.VMEM((16, 5, 8, 128), F32),
            pltpu.VMEM((2,) + plane, F32),
            pltpu.VMEM((ROWS, COLS), F32),
            pltpu.VMEM((STEPS, ROWS, COLS), F32),
            pltpu.VMEM((STEPS,) + plane, BF16),
            pltpu.VMEM((STEPS,) + plane, BF16),
            pltpu.VMEM((STEPS, 2, 8, 128), F32),
            pltpu.VMEM((STEPS, 2, 8, 128), F32),
            dma((NF, 2)),
            dma((NF - 1, 2)),
            dma((NF, 2)),
            dma((NS,)),
            dma((16,)),
            dma((STEPS, 2)),
            dma((STEPS, 2)),
            dma((STEPS, 2)),
            dma((STEPS, 2)),
        ],
        compiler_params=pltpu.CompilerParams(
            collective_id=0, has_side_effects=True, vmem_limit_bytes=48 * 2**20
        ),
        name="window",
    )(
        previous_field, current_field, courant, wavelet, traces, source_cell,
        receiver_cells.reshape(1, -1), spectra,
    )


HALF = 16


def image_kernel(lag_ref, mix_ref, planes, fresh, out, early, late):
    lanes = lax.broadcasted_iota(jnp.int32, (HALF, 128), 1)
    columns = lax.broadcasted_iota(jnp.int32, (HALF, COLS), 1)
    terms = NF * TERMS
    weight = 1.0 / (STEPS * terms / 2)

    for half in range(ROWS // HALF):
        rows = pl.ds(half * HALF, HALF)
        for w, held in ((0, early), (1, late)):
            snaps = planes[pl.ds(1, STEPS), w, rows, :].reshape(STEPS * HALF, COLS)

            def gather(g, carry, w=w, held=held, snaps=snaps, rows=rows):
                part = jnp.dot(
                    mix_ref[pl.ds(pl.multiple_of(g * TERMS * HALF, TERMS * HALF), TERMS * HALF), :],
                    snaps, preferred_element_type=F32,
                )
                total = part.reshape(TERMS, HALF, COLS) + fresh[g, w, :, rows, :].astype(F32)
                if w == 1:
                    total = pltpu.roll(total, 2 * LAGMAX, 2)
                held[pl.ds(g * TERMS, TERMS)] = total
                return carry

            lax.fori_loop(0, NF, gather, 0)

        def one_lag(h, carry, rows=rows, half=half):
            lag = lag_ref[h]
            ahead = 2 * lag + 2 * LAGMAX
            back = lax.rem(128 - ahead, 128)
            inside = lanes < 128 - ahead

            def add(k, sums):
                for i in range(4):
                    term = k * 4 + i
                    turned = [
                        pltpu.roll(late[term, :, pl.ds(128 * c, 128)], back, 1) for c in range(4)
                    ]
                    sums = tuple(
                        sums[c]
                        + early[term, :, pl.ds(128 * c, 128)]
                        * jnp.where(inside, turned[c], turned[(c + 1) % 4])
                        for c in range(4)
                    )
                return sums

            sums = lax.fori_loop(
                0, terms // 4, add, tuple(jnp.zeros((HALF, 128), F32) for _ in range(4))
            )
            total = jnp.concatenate(sums, axis=1) * weight
            total = pltpu.roll(total, COLS - LAGMAX, 1)
            forward = lag + LAGMAX
            turned = [pltpu.roll(total[:, 128 * c : 128 * (c + 1)], forward, 1) for c in range(4)]
            moved = jnp.concatenate(
                [jnp.where(lanes < forward, turned[(c + 3) % 4], turned[c]) for c in range(4)], axis=1
            )
            reach = jnp.abs(lag)
            kept = jnp.where((columns >= reach) & (columns < COLS - reach), moved, 0.0)
            out[h, rows, :] = kept.astype(BF16)
            return carry

        lax.fori_loop(0, lag_ref.shape[0], one_lag, 0)


def make_image(lag_list, mix, planes, fresh):
    vmem = pl.BlockSpec(memory_space=pltpu.VMEM)
    lags = lag_list.shape[0]
    return pl.pallas_call(
        image_kernel,
        out_shape=jax.ShapeDtypeStruct((lags, ROWS, COLS), BF16),
        in_specs=[pl.BlockSpec(memory_space=pltpu.SMEM), vmem, vmem, vmem],
        out_specs=vmem,
        scratch_shapes=[
            pltpu.VMEM((NF * TERMS, HALF, COLS), F32),
            pltpu.VMEM((NF * TERMS, HALF, COLS), F32),
        ],
        compiler_params=pltpu.CompilerParams(vmem_limit_bytes=48 * 2**20),
        name="image",
    )(lag_list, mix, planes, fresh)


def body(
    previous_field, current_field, courant, wavelet, traces, source_cell, receiver_cells,
    frequency_list, lag_list, spectra,
):
    table = dft_table(frequency_list).reshape(STEPS, NF * TERMS)
    same = jnp.eye(HALF, dtype=BF16)
    mix = (table.T[:, None, :, None] * same[None, :, None, :]).reshape(NF * TERMS * HALF, STEPS * HALF)
    planes, fresh = window(
        previous_field, current_field, courant, wavelet, traces, source_cell, receiver_cells,
        spectra.reshape(2, TERMS, NY, COLS),
    )
    image = make_image(lag_list, mix, planes, fresh)
    return image.reshape(lag_list.shape[0], 1, 1, ROWS, COLS)


def solution(mesh):
    placed = (
        P(None, "xy", "slab", "freq"),
        P(None, "xy", "slab", "freq"),
        P("xy", "slab", "freq"),
        P(),
        P(),
        P(),
        P(),
        P(),
        P(),
        P(None, "freq", None, "xy", "slab", None, None),
    )
    return jax.shard_map(
        body,
        mesh=mesh,
        in_specs=placed,
        out_specs=P(None, "xy", "slab", "freq", None),
        check_vma=False,
    )
```

time: 1130 us -> 302 us (0.27)
  the two profiles are of different devices: /device:TPU:1 before, /device:TPU:63 now
where the time goes in v1:
time: 302 us; the launch traced here: 301 us
  Pallas kernels  292 us (97%)
  local copies, waits for them, and re-layouts  5.61 us (2%)
  other arithmetic  3.08 us (1%)
    pallas_call x1, Pallas kernels, window(): pl.pallas_call(window_kernel, out_shape=(jax.ShapeDtypeStruct((STEPS + 1,...  225 us
    pallas_call x1, Pallas kernels, make_image(): pl.pallas_call(image_kernel, out_shape=jax.ShapeDtypeStruct((lags, ROWS,...  67.2 us

profile of v1, /device:TPU:63, one launch (start us, length us, event | category | flops | bytes accessed | tf_op | source)
XLA Modules:
  0.0 301.4 jit_solution(3388563485234088267)
XLA Ops:
  0.7 0.8 cosine_convert_fusion
  1.5 0.1 copy.14
  1.6 0.0 copy-start
  1.6 0.0 copy-start.1
  1.6 0.0 copy-start.2
  1.6 0.0 copy-start.3
  1.6 0.0 copy-start.4
  1.6 0.0 copy-start.5
  1.6 2.3 broadcast_multiply_fusion
  3.9 5.5 %mul.66.mix_ref = bf16[1024,256]{1,0:T(8,128)(2,1)S(1)} reshape(bf16[64,16,16,16]{3,2,1,0:T(8,128)(2,1)} %broadcast_multiply_fusion) | data formatting | bytes 1048576 | tf_op jit(solution)/shard_map/mul | solution.py:460
  9.4 0.0 copy-done
  9.4 0.0 copy-done.1
  9.4 0.0 copy-done.2
  9.4 0.0 copy-done.3
  9.4 0.0 copy-done.4
  9.5 0.0 copy-done.5
  9.5 0.0 copy-start.6
  9.5 224.7 %window.1 = (bf16[17,2,32,512]{3,2,1,0:T(8,128)(2,1)S(1)}, bf16[4,2,16,32,512]{4,3,2,1,0:T(8,128)(2,1)S(1)}) custom-call(f32[2,16,8,128]{3,2,1,0:T(8,128)S(1)} %copy-done, f32[2,16,8,128]{3,2,1,0:T(8,128)S(1)} %copy-done.1, f32[16,8,128]{2,1,0:T(8,128)S(1)} %copy-done.2, f32[16]{0:T(128)S(1)} %copy-done.5, f32[16,256]{1,0:T(8,128)S(1)} %copy-done.3, ...), custom_call_target="tpu_custom_call" | custom-call | tf_op jit(solution)/shard_map/window/pallas_call | solution.py:332
  234.2 0.0 copy-done.6
  234.2 67.2 %image.1 = bf16[17,32,512]{2,1,0:T(8,128)(2,1)} custom-call(s32[17]{0:T(128)S(1)} %copy-done.6, bf16[1024,256]{1,0:T(8,128)(2,1)S(1)} %mul.66.mix_ref, bf16[17,2,32,512]{3,2,1,0:T(8,128)(2,1)S(1)} %get-tuple-element.7.planes, bf16[4,2,16,32,512]{4,3,2,1,0:T(8,128)(2,1)S(1)} %get-tuple-element.8.fresh), custom_call_target="tpu_custom_call" | custom-call | tf_op jit(solution)/shard_map/image/pallas_call | solution.py:440
  (3 shorter events, 0.0 us)
Async XLA Ops:
  1.6 7.8 %copy-start = (f32[2,16,8,128]{3,2,1,0:T(8,128)S(1)}, f32[2,16,8,128]{3,2,1,0:T(8,128)}, u32[]{:S(2)}) copy-start(f32[2,16,8,128]{3,2,1,0:T(8,128)} %prev_ref.1) | copy-start | bytes 393220
  1.6 7.8 %copy-start.1 = (f32[2,16,8,128]{3,2,1,0:T(8,128)S(1)}, f32[2,16,8,128]{3,2,1,0:T(8,128)}, u32[]{:S(2)}) copy-start(f32[2,16,8,128]{3,2,1,0:T(8,128)} %cur_ref.1) | copy-start | bytes 393220
  1.6 7.8 %copy-start.2 = (f32[16,8,128]{2,1,0:T(8,128)S(1)}, f32[16,8,128]{2,1,0:T(8,128)}, u32[]{:S(2)}) copy-start(f32[16,8,128]{2,1,0:T(8,128)} %cour_ref.1) | copy-start | bytes 196612
  1.6 7.8 %copy-start.3 = (f32[16,256]{1,0:T(8,128)S(1)}, f32[16,256]{1,0:T(8,128)}, u32[]{:S(2)}) copy-start(f32[16,256]{1,0:T(8,128)} %traces_ref.1) | copy-start | bytes 49156
  1.6 7.8 %copy-start.4 = (s32[256]{0:T(256)S(1)}, s32[256]{0:T(256)}, u32[]{:S(2)}) copy-start(s32[256]{0:T(256)} %param.16) | copy-start | bytes 3076
  1.6 7.8 %copy-start.5 = (f32[16]{0:T(128)S(1)}, f32[16]{0:T(128)}, u32[]{:S(2)}) copy-start(f32[16]{0:T(128)} %wav_ref.1) | copy-start | bytes 196
  9.5 224.8 %copy-start.6 = (s32[17]{0:T(128)S(1)}, s32[17]{0:T(128)}, u32[]{:S(2)}) copy-start(s32[17]{0:T(128)} %lag_ref.1) | copy-start | bytes 208

commit v2 on v0

v2 whole, which is shorter than its diff:
```python
import math

import jax
import jax.numpy as jnp
from jax import lax
from jax.experimental import pallas as pl
from jax.experimental.pallas import tpu as pltpu
from jax.sharding import PartitionSpec as P

STEPS = 16
NTOT = 2048
LAGMAX = 16
NF, NS, NB = 4, 16, 4
ROWS, COLS = 32, 512
DEEP, WIDE = 4, 8
TERMS = 16
NY = NF * ROWS
F32, BF16 = jnp.float32, jnp.bfloat16
XS = 128
BLOCKS = COLS // XS
HALF = 16
ROUND = 4
BESIDE = 10
MESH = pl.DeviceIdType.MESH


def dft_table(frequency_list):
    moments = jnp.arange(STEPS, dtype=jnp.int32) + (NTOT - STEPS)
    phase_index = moments[:, None] * frequency_list[None, :] % NTOT
    phase_angle = phase_index.astype(F32) * (2.0 * math.pi / NTOT)
    return jnp.stack([jnp.cos(phase_angle), -jnp.sin(phase_angle)], axis=-1).astype(BF16)


def turned(rows):
    return jnp.concatenate([rows[:, XS * c : XS * (c + 1)] for c in range(BLOCKS)], axis=0).T


def kernel(
    prev_ref, cur_ref, cour_ref, wav_ref, traces_ref, src_ref, rec_ref, lag_ref, table_ref, spec_ref,
    out,
    raw, outgoing, fresh, pieces_out, pieces_in, field, cour, inj, planes, held, lo, hi, yout, yin,
    spread, mix, snaps, early, late, sums,
    raw_sem, spec_send, spec_recv, piece_send, piece_recv,
    zsend, zrecv, ysend, yrecv, held_send, held_recv,
):
    f, j, b = lax.axis_index("freq"), lax.axis_index("slab"), lax.axis_index("xy")
    deep, wide = j // 4, j % 4
    layer, strip = b * 4 + deep, f * 4 + wide
    first_plane, first_row = layer * DEEP, strip * WIDE
    has_lo, has_hi = layer > 0, layer < NB * 4 - 1
    has_top, has_bottom = strip > 0, strip < NF * 4 - 1
    lags = lag_ref.shape[0]

    def layer_at(other):
        return {"freq": f, "slab": (other % 4) * 4 + wide, "xy": other // 4}

    def strip_at(other):
        return {"freq": other // 4, "slab": deep * 4 + other % 4, "xy": b}

    def group_at(other):
        return {"freq": other, "slab": j, "xy": b}

    def plane_at(other):
        return {"freq": f, "slab": deep * 4 + other, "xy": b}

    peers = (lax.rem(f + 2, NF), NF - 1 - f, f + 1 - 2 * lax.rem(f, 2))
    chunk = peers + (f,)
    mates = tuple(lax.rem(wide + n, 4) for n in (1, 2, 3))

    def raw_copy(o, w):
        return pltpu.make_async_copy(
            spec_ref.at[w, :, pl.ds(chunk[o] * ROWS, ROWS), :], raw.at[o, w], raw_sem.at[o, w]
        )

    for o in range(NF):
        for w in range(2):
            raw_copy(o, w).start()

    barrier = pltpu.get_barrier_semaphore()
    mine = deep == f

    def greet(there):
        pl.semaphore_signal(barrier, 1, device_id=there, device_id_type=MESH)

    for p in peers:
        greet(group_at(p))
    for m in mates:
        greet(plane_at(m))
    for present, there in (
        (has_lo, layer_at(layer - 1)), (has_hi, layer_at(layer + 1)),
        (has_top, strip_at(strip - 1)), (has_bottom, strip_at(strip + 1)),
    ):
        @pl.when(present)
        def _(there=there):
            greet(there)

    for f0 in range(NF):
        @pl.when(jnp.logical_not(mine & (f == f0)))
        def _(f0=f0):
            greet({"freq": f0, "slab": 4 * f + wide, "xy": b})

    def stack(i, carry):
        group, p = i // DEEP, i % DEEP
        for w in range(2):
            pieces_out[group, w, p] = prev_ref[w, i]
            pieces_out[group, 2 + w, p] = cur_ref[w, i]
        pieces_out[group, 4, p] = cour_ref[i]
        return carry

    lax.fori_loop(0, NS, stack, 0)

    expected = len(peers) + len(mates) + NF - mine.astype(jnp.int32)
    for present in (has_lo, has_hi, has_top, has_bottom):
        expected += present.astype(jnp.int32)
    pl.semaphore_wait(barrier, expected)

    def piece_copy(group):
        return pltpu.make_async_remote_copy(
            src_ref=pieces_out.at[group],
            dst_ref=pieces_in.at[f],
            send_sem=piece_send.at[group],
            recv_sem=piece_recv.at[f],
            device_id={"freq": deep, "slab": 4 * group + wide, "xy": b},
            device_id_type=MESH,
        )

    for group in range(4):
        @pl.when(jnp.logical_not(mine & (deep == group)))
        def _(group=group):
            piece_copy(group).start()

    @pl.when(mine)
    def _():
        pieces_in[f] = pieces_out[deep]

    cell = rec_ref[...]
    depth, row, col = (cell >> 16) - first_plane, ((cell >> 9) & (NY - 1)) - first_row, cell & (COLS - 1)
    here = (depth >= 0) & (depth < DEEP) & (row >= 0) & (row < WIDE)
    row = jnp.where(here, depth * WIDE + row, -1)
    at_row = lax.broadcasted_iota(jnp.int32, (ROWS, cell.shape[1]), 0) == row
    at_col = (lax.broadcasted_iota(jnp.int32, (COLS, cell.shape[1]), 0) == col).astype(F32).astype(BF16)

    def inject(t, carry):
        values = jnp.where(at_row, traces_ref[pl.ds(t, 1), :], 0.0)
        first = values.astype(BF16)
        rest = values - first.astype(F32)
        second = rest.astype(BF16)
        third = (rest - second.astype(F32)).astype(BF16)
        parts = lax.dot_general(
            jnp.concatenate([first, second, third], axis=0), at_col,
            (((1,), (1,)), ((), ())), preferred_element_type=F32,
        )
        inj[t] = (parts[:ROWS] + parts[ROWS : 2 * ROWS] + parts[2 * ROWS :]).reshape(DEEP, WIDE, COLS)
        return carry

    lax.fori_loop(0, STEPS, inject, 0)

    terms = NF * TERMS
    step_of = lax.broadcasted_iota(jnp.int32, (STEPS, STEPS * HALF), 1) // HALF
    chosen = (step_of == lax.broadcasted_iota(jnp.int32, (STEPS, STEPS * HALF), 0)).astype(F32).astype(BF16)
    spread[...] = jnp.dot(table_ref[...], chosen, preferred_element_type=F32)
    place = lax.broadcasted_iota(jnp.int32, (HALF, STEPS * HALF), 1) % HALF
    diagonal = place == lax.broadcasted_iota(jnp.int32, (HALF, STEPS * HALF), 0)

    def fill(k, carry):
        values = jnp.where(diagonal, spread[pl.ds(k, 1), :], 0.0)
        mix[pl.ds(pl.multiple_of(k * HALF, HALF), HALF), :] = values.astype(BF16)
        return carry

    lax.fori_loop(0, terms, fill, 0)

    for o in range(NF):
        for w in range(2):
            raw_copy(o, w).wait()

    row_id = lax.broadcasted_iota(jnp.int32, (WIDE, COLS), 0)
    col_id = lax.broadcasted_iota(jnp.int32, (WIDE, COLS), 1)

    for f0 in range(NF):
        @pl.when(jnp.logical_not(mine & (f == f0)))
        def _(f0=f0):
            pltpu.make_async_remote_copy(
                src_ref=pieces_out.at[0], dst_ref=pieces_in.at[f0],
                send_sem=piece_send.at[0], recv_sem=piece_recv.at[f0],
                device_id=group_at(f), device_id_type=MESH,
            ).wait_recv()

        cols = pl.ds(128 * f0, 128)
        for p in range(DEEP):
            for w in range(2):
                field[1, p, w, :, cols] = pieces_in[f0, w, p]
                field[0, p, w, :, cols] = pieces_in[f0, 2 + w, p]
            cour[p, :, cols] = pieces_in[f0, 4, p]

    def z_copy(s, up):
        return pltpu.make_async_remote_copy(
            src_ref=planes.at[s, DEEP - 1 if up else 0],
            dst_ref=(lo if up else hi).at[s],
            send_sem=zsend.at[s, int(up)],
            recv_sem=zrecv.at[s, int(up)],
            device_id=layer_at(layer + 1 if up else layer - 1),
            device_id_type=MESH,
        )

    def y_copy(s, down):
        return pltpu.make_async_remote_copy(
            src_ref=yout.at[s, int(down)],
            dst_ref=yin.at[s, int(down)],
            send_sem=ysend.at[s, int(down)],
            recv_sem=yrecv.at[s, int(down)],
            device_id=strip_at(strip + 1 if down else strip - 1),
            device_id_type=MESH,
        )

    directions = (
        (has_hi, z_copy, True), (has_lo, z_copy, False), (has_bottom, y_copy, True), (has_top, y_copy, False)
    )

    def publish(s, p, values):
        planes[s, p] = jnp.concatenate(values, axis=0).astype(BF16)
        for w in range(2):
            yout[s, 0, pl.ds(2 * p + w, 1), :] = values[w][0:1]
            yout[s, 1, pl.ds(2 * p + w, 1), :] = values[w][WIDE - 1 : WIDE]

    def send(s):
        for present, copy, forward in directions:
            @pl.when(present)
            def _(copy=copy, forward=forward):
                copy(s, forward).start()

    def spec_copy(o, k):
        return pltpu.make_async_remote_copy(
            src_ref=outgoing.at[o, k],
            dst_ref=fresh.at[f, k],
            send_sem=spec_send.at[o, k],
            recv_sem=spec_recv.at[f, k],
            device_id=group_at(peers[o]),
            device_id_type=MESH,
        )

    def send_spectra(k):
        for o in range(NF - 1):
            for w in range(2):
                outgoing[o, k, w] = turned(raw[o, w, k]).astype(BF16)
            spec_copy(o, k).start()
        for w in range(2):
            fresh[f, k, w] = turned(raw[NF - 1, w, k]).astype(BF16)

    def held_copy(n, batch):
        return pltpu.make_async_remote_copy(
            src_ref=planes.at[pl.ds(4 * batch + 1, 4), mates[n]],
            dst_ref=held.at[pl.ds(4 * batch, 4), wide],
            send_sem=held_send.at[batch, n],
            recv_sem=held_recv.at[batch, wide],
            device_id=plane_at(mates[n]),
            device_id_type=MESH,
        )

    for p in range(DEEP):
        publish(0, p, [field[0, p, w] for w in range(2)])
    send(0)

    source = src_ref[0]
    source_row = ((source >> 9) & (NY - 1)) - first_row
    source_plane = (source >> 16) - first_plane
    at_source = (row_id == source_row) & (col_id == (source & (COLS - 1)))

    def arrivals(s, present, copy, there):
        @pl.when(present)
        def _():
            copy.wait_recv()

        @pl.when(jnp.logical_not(present))
        def _():
            there[s] = jnp.zeros(there.shape[1:], there.dtype)

    def advance(t, carry):
        now, other = t % 2, (t + 1) % 2

        @pl.when(t < BESIDE)
        def _():
            send_spectra(t)

        arrivals(t, has_lo, z_copy(t, True), lo)
        arrivals(t, has_hi, z_copy(t, False), hi)
        arrivals(t, has_top, y_copy(t, True), yin.at[:, 1])
        arrivals(t, has_bottom, y_copy(t, False), yin.at[:, 0])
        below = [lo[t].astype(F32)[WIDE * w : WIDE * (w + 1)] for w in range(2)]
        above = [hi[t].astype(F32)[WIDE * w : WIDE * (w + 1)] for w in range(2)]
        for p in range(DEEP):
            values = []
            for w in range(2):
                u = field[now, p, w]
                beside = (field[now, p - 1, w] if p else below[w])
                beside += (field[now, p + 1, w] if p < DEEP - 1 else above[w])
                top, bottom = (yin[t, d, pl.ds(2 * p + w, 1), :] for d in (1, 0))
                beside += jnp.where(row_id == 0, top, pltpu.roll(u, 1, 0))
                beside += jnp.where(row_id == WIDE - 1, bottom, pltpu.roll(u, WIDE - 1, 0))
                beside += jnp.where(col_id == 0, 0.0, pltpu.roll(u, 1, 1))
                beside += jnp.where(col_id == COLS - 1, 0.0, pltpu.roll(u, COLS - 1, 1))
                if w == 1:
                    injection = inj[t, p]
                else:
                    injection = jnp.where(at_source & (source_plane == p), wav_ref[t], 0.0)
                following = 2.0 * u - field[other, p, w] + cour[p] * (beside - 6.0 * u) + injection
                field[other, p, w] = following
                values.append(following)
            publish(t + 1, p, values)

        @pl.when(t < STEPS - 1)
        def _():
            send(t + 1)

        held[t, wide] = planes[t + 1, wide]

        @pl.when(t % 4 == 3)
        def _():
            for n in range(3):
                held_copy(n, t // 4).start()

        return carry

    lax.fori_loop(0, STEPS, advance, 0)

    def rest(k, carry):
        send_spectra(k)
        return carry

    lax.fori_loop(BESIDE, TERMS, rest, 0)

    def turn_batch(batch, carry):
        for n in range(3):
            pltpu.make_async_remote_copy(
                src_ref=planes.at[pl.ds(4 * batch + 1, 4), mates[n]],
                dst_ref=held.at[pl.ds(4 * batch, 4), mates[n]],
                send_sem=held_send.at[batch, n], recv_sem=held_recv.at[batch, mates[n]],
                device_id=plane_at(mates[n]), device_id_type=MESH,
            ).wait_recv()

        def turn(q, inner):
            t = 4 * batch + q
            strips = held[t].astype(F32)
            for w in range(2):
                plane = turned(strips[:, WIDE * w : WIDE * (w + 1)].reshape(ROWS, COLS)).astype(BF16)
                for i in range(XS // HALF):
                    snaps[w, i // 2, t, :, pl.ds((i % 2) * XS, XS)] = plane[HALF * i : HALF * (i + 1)]
            return inner

        return lax.fori_loop(0, 4, turn, carry)

    lax.fori_loop(0, STEPS // 4, turn_batch, 0)

    offsets = [2 * lag_ref[h] + 2 * LAGMAX for h in range(lags)]
    batch = ROUND * NF

    def clear(h, carry):
        sums[h] = jnp.zeros(sums.shape[1:], F32)
        return carry

    lax.fori_loop(0, lags, clear, 0)

    def one_round(r, carry):
        def arrive(q, inner):
            k = r * ROUND + q
            for o in range(NF - 1):
                pltpu.make_async_remote_copy(
                    src_ref=outgoing.at[o, k], dst_ref=fresh.at[peers[o], k],
                    send_sem=spec_send.at[o, k], recv_sem=spec_recv.at[peers[o], k],
                    device_id=group_at(peers[o]), device_id_type=MESH,
                ).wait_recv()
            return inner

        lax.fori_loop(0, ROUND, arrive, 0)
        size = batch * HALF
        table = mix[pl.ds(pl.multiple_of(r * size, size), size), :]
        for w in range(2):
            for pair in range(XS // HALF // 2):
                moments = snaps[w, pair].reshape(STEPS * HALF, 2 * XS)
                part = jnp.dot(table, moments, preferred_element_type=F32).reshape(batch, HALF, 2 * XS)
                for q in range(ROUND):
                    for g in range(NF):
                        for i in range(2):
                            at = HALF * (2 * pair + i)
                            total = part[q * NF + g, :, XS * i : XS * (i + 1)]
                            total += fresh[g, r * ROUND + q, w, pl.ds(at, HALF), :].astype(F32)
                            if w == 0:
                                early[q * NF + g, pl.ds(at, HALF), :] = total
                            else:
                                late[q * NF + g, pl.ds(at + 2 * LAGMAX, HALF), :] = total

        def wrap(k, inner):
            late[k, pl.ds(0, 2 * LAGMAX), :] = pltpu.roll(late[k, pl.ds(XS, 2 * LAGMAX), :], ROWS, 1)
            late[k, pl.ds(XS + 2 * LAGMAX, 2 * LAGMAX), :] = pltpu.roll(
                late[k, pl.ds(2 * LAGMAX, 2 * LAGMAX), :], XS - ROWS, 1
            )
            return inner

        lax.fori_loop(0, batch, wrap, 0)

        def tile(i, inner):
            at = pl.multiple_of(i * HALF, HALF)
            starts = [at + offset for offset in offsets]

            def add(k, totals):
                for step in range(4):
                    one = early[4 * k + step, pl.ds(at, HALF), :]
                    totals = tuple(
                        total + one * late[4 * k + step, pl.ds(start, HALF), :]
                        for total, start in zip(totals, starts)
                    )
                return totals

            totals = lax.fori_loop(
                0, batch // 4, add, tuple(sums[h, pl.ds(at + LAGMAX, HALF), :] for h in range(lags))
            )
            for h in range(lags):
                sums[h, pl.ds(at + LAGMAX, HALF), :] = totals[h]
            return inner

        return lax.fori_loop(0, XS // HALF, tile, carry)

    lax.fori_loop(0, TERMS // ROUND, one_round, 0)

    x = (
        lax.broadcasted_iota(jnp.int32, (XS, XS), 0)
        + lax.broadcasted_iota(jnp.int32, (XS, XS), 1) // ROWS * XS
    )
    weight = 1.0 / (STEPS * terms / 2)

    def finish(h, carry):
        lag = lag_ref[h]
        sums[h, pl.ds(0, LAGMAX), :] = pltpu.roll(sums[h, pl.ds(XS, LAGMAX), :], ROWS, 1)
        sums[h, pl.ds(XS + LAGMAX, LAGMAX), :] = pltpu.roll(sums[h, pl.ds(LAGMAX, LAGMAX), :], XS - ROWS, 1)
        moved = sums[h, pl.ds(LAGMAX - lag, XS), :]
        reach = jnp.abs(lag)
        kept = jnp.where((x >= reach) & (x < COLS - reach), moved * weight, 0.0).T
        for c in range(BLOCKS):
            out[h, :, pl.ds(XS * c, XS)] = kept[ROWS * c : ROWS * (c + 1)].astype(BF16)
        return carry

    lax.fori_loop(0, lags, finish, 0)

    def sent(s, carry):
        for present, copy, forward in directions:
            @pl.when(present)
            def _(copy=copy, forward=forward):
                copy(s, forward).wait_send()

        for o in range(NF - 1):
            spec_copy(o, s).wait_send()
        return carry

    lax.fori_loop(0, STEPS, sent, 0)

    def delivered(batch, carry):
        for n in range(3):
            held_copy(n, batch).wait_send()
        return carry

    lax.fori_loop(0, STEPS // 4, delivered, 0)

    for group in range(4):
        @pl.when(jnp.logical_not(mine & (deep == group)))
        def _(group=group):
            piece_copy(group).wait_send()


def body(
    previous_field, current_field, courant, wavelet, traces, source_cell, receiver_cells,
    frequency_list, lag_list, spectra,
):
    lags, terms = lag_list.shape[0], NF * TERMS
    table = dft_table(frequency_list).reshape(STEPS, NF, TERMS).transpose(2, 1, 0).reshape(terms, STEPS)
    vmem = pl.BlockSpec(memory_space=pltpu.VMEM)
    smem = pl.BlockSpec(memory_space=pltpu.SMEM)
    dma = pltpu.SemaphoreType.DMA
    pair = (2 * WIDE, COLS)
    image = pl.pallas_call(
        kernel,
        out_shape=jax.ShapeDtypeStruct((lags, ROWS, COLS), BF16),
        in_specs=[vmem, vmem, vmem, smem, vmem, smem, vmem, smem, vmem, pl.BlockSpec(memory_space=pl.ANY)],
        out_specs=vmem,
        scratch_shapes=[
            pltpu.VMEM((NF, 2, TERMS, ROWS, COLS), F32),
            pltpu.VMEM((NF - 1, TERMS, 2, XS, XS), BF16),
            pltpu.VMEM((NF, TERMS, 2, XS, XS), BF16),
            pltpu.VMEM((4, 5, DEEP, WIDE, 128), F32),
            pltpu.VMEM((NF, 5, DEEP, WIDE, 128), F32),
            pltpu.VMEM((2, DEEP, 2, WIDE, COLS), F32),
            pltpu.VMEM((DEEP, WIDE, COLS), F32),
            pltpu.VMEM((STEPS, DEEP, WIDE, COLS), F32),
            pltpu.VMEM((STEPS + 1, DEEP) + pair, BF16),
            pltpu.VMEM((STEPS, 4) + pair, BF16),
            pltpu.VMEM((STEPS,) + pair, BF16),
            pltpu.VMEM((STEPS,) + pair, BF16),
            pltpu.VMEM((STEPS + 1, 2, 2 * DEEP, COLS), F32),
            pltpu.VMEM((STEPS, 2, 2 * DEEP, COLS), F32),
            pltpu.VMEM((terms, STEPS * HALF), F32),
            pltpu.VMEM((terms * HALF, STEPS * HALF), BF16),
            pltpu.VMEM((2, XS // HALF // 2, STEPS, HALF, 2 * XS), BF16),
            pltpu.VMEM((ROUND * NF, XS, XS), F32),
            pltpu.VMEM((ROUND * NF, XS + 4 * LAGMAX, XS), F32),
            pltpu.VMEM((lags, XS + 2 * LAGMAX, XS), F32),
            dma((NF, 2)),
            dma((NF - 1, TERMS)),
            dma((NF, TERMS)),
            dma((4,)),
            dma((NF,)),
            dma((STEPS, 2)),
            dma((STEPS, 2)),
            dma((STEPS, 2)),
            dma((STEPS, 2)),
            dma((STEPS // 4, 3)),
            dma((STEPS // 4, 4)),
        ],
        compiler_params=pltpu.CompilerParams(
            collective_id=0, has_side_effects=True, vmem_limit_bytes=56 * 2**20
        ),
        name="window_image",
    )(
        previous_field, current_field, courant, wavelet, traces, source_cell,
        receiver_cells.reshape(1, -1), lag_list, table, spectra.reshape(2, TERMS, NY, COLS),
    )
    return image.reshape(lags, 1, 1, ROWS, COLS)


def solution(mesh):
    placed = (
        P(None, "xy", "slab", "freq"),
        P(None, "xy", "slab", "freq"),
        P("xy", "slab", "freq"),
        P(),
        P(),
        P(),
        P(),
        P(),
        P(),
        P(None, "freq", None, "xy", "slab", None, None),
    )
    return jax.shard_map(
        body,
        mesh=mesh,
        in_specs=placed,
        out_specs=P(None, "xy", "slab", "freq", None),
        check_vma=False,
    )
```

time: 1130 us -> 162 us (0.14)
  the two profiles are of different devices: /device:TPU:1 before, /device:TPU:25 now
where the time goes in v2:
time: 162 us
  Pallas kernels  158 us (98%)
  local copies, waits for them, and re-layouts  2.61 us (2%)
    pallas_call x1, Pallas kernels, body(): pl.pallas_call(kernel, out_shape=jax.ShapeDtypeStruct((lags, ROWS, COLS),...  158 us

profile of v2, /device:TPU:25, one launch (start us, length us, event | category | flops | bytes accessed | tf_op | source)
XLA Modules:
  0.0 162.1 jit_solution(8746686030127056485)
XLA Ops:
  0.7 0.8 cosine_convert_fusion
  1.5 0.1 copy.14
  1.6 0.6 copy.15
  2.2 158.0 %window_image.1 = bf16[17,32,512]{2,1,0:T(8,128)(2,1)} custom-call(f32[2,16,8,128]{3,2,1,0:T(8,128)} %prev_ref.1, f32[2,16,8,128]{3,2,1,0:T(8,128)} %cur_ref.1, f32[16,8,128]{2,1,0:T(8,128)} %cour_ref.1, f32[16]{0:T(128)} %wav_ref.1, f32[16,256]{1,0:T(8,128)} %traces_ref.1, s32[1]{0:T(128)S(6)} %copy.18.src_ref, s32[1,256]{1,0:T(1,128)} %bitcast.13, ...), custom_call_target="tpu_custom_call" | custom-call | tf_op jit(solution)/shard_map/window_image/pallas_call | solution.py:478
  160.2 1.9 %copy.19 = bf16[17,1,1,32,512]{4,3,2,1,0:T(8,128)(2,1)} copy(bf16[17,1,1,32,512]{4,3,2,1,0:T(8,128)(2,1)} %bitcast.10) | data formatting | bytes 1114112
  (2 shorter events, 0.0 us)

commit v3 on v2

--- a/solution.py
+++ b/solution.py
@@ -13,14 +13,16 @@
 NF, NS, NB = 4, 16, 4
 ROWS, COLS = 32, 512
 DEEP, WIDE = 4, 8
+RING = 16
 TERMS = 16
 NY = NF * ROWS
 F32, BF16 = jnp.float32, jnp.bfloat16
 XS = 128
 BLOCKS = COLS // XS
 HALF = 16
-ROUND = 4
-BESIDE = 10
+ROUND = 2
+ROUNDS = STEPS // 2
+AHEAD, EACH, BESIDE = 2, 1, 10
 MESH = pl.DeviceIdType.MESH
 
 
@@ -31,6 +33,10 @@
     return jnp.stack([jnp.cos(phase_angle), -jnp.sin(phase_angle)], axis=-1).astype(BF16)
 
 
+def swung(outer, inner):
+    return inner + outer % 2 * (3 - 2 * inner)
+
+
 def turned(rows):
     return jnp.concatenate([rows[:, XS * c : XS * (c + 1)] for c in range(BLOCKS)], axis=0).T
 
@@ -38,24 +44,27 @@
 def kernel(
     prev_ref, cur_ref, cour_ref, wav_ref, traces_ref, src_ref, rec_ref, lag_ref, table_ref, spec_ref,
     out,
-    raw, outgoing, fresh, pieces_out, pieces_in, field, cour, inj, planes, held, lo, hi, yout, yin,
+    raw, outgoing, fresh, pieces_out, pieces_in, field, cour, inj, planes, held, lo, hi, yout, yin, corner_out, corner, first_z, first_y, first_lo, first_hi, first_in,
     spread, mix, snaps, early, late, sums,
     raw_sem, spec_send, spec_recv, piece_send, piece_recv,
-    zsend, zrecv, ysend, yrecv, held_send, held_recv,
+    zsend, zrecv, ysend, yrecv, csend, crecv, fsend, frecv, held_send, held_recv,
 ):
     f, j, b = lax.axis_index("freq"), lax.axis_index("slab"), lax.axis_index("xy")
-    deep, wide = j // 4, j % 4
+    home, post = j // 4, j % 4
+    deep, wide = swung(b, home), swung(f, post)
     layer, strip = b * 4 + deep, f * 4 + wide
     first_plane, first_row = layer * DEEP, strip * WIDE
     has_lo, has_hi = layer > 0, layer < NB * 4 - 1
     has_top, has_bottom = strip > 0, strip < NF * 4 - 1
     lags = lag_ref.shape[0]
 
-    def layer_at(other):
-        return {"freq": f, "slab": (other % 4) * 4 + wide, "xy": other // 4}
-
-    def strip_at(other):
-        return {"freq": other // 4, "slab": deep * 4 + other % 4, "xy": b}
+    def block_at(up, down):
+        to_layer, to_strip = layer + up, strip + down
+        return {
+            "freq": to_strip // 4,
+            "slab": swung(to_layer // 4, to_layer % 4) * 4 + swung(to_strip // 4, to_strip % 4),
+            "xy": to_layer // 4,
+        }
 
     def group_at(other):
         return {"freq": other, "slab": j, "xy": b}
@@ -65,7 +74,7 @@
 
     peers = (lax.rem(f + 2, NF), NF - 1 - f, f + 1 - 2 * lax.rem(f, 2))
     chunk = peers + (f,)
-    mates = tuple(lax.rem(wide + n, 4) for n in (1, 2, 3))
+    owns = b % 2 == 0
 
     def raw_copy(o, w):
         return pltpu.make_async_copy(
@@ -77,22 +86,27 @@
             raw_copy(o, w).start()
 
     barrier = pltpu.get_barrier_semaphore()
-    mine = deep == f
+    mine = (home == f) & (f % 2 == 0)
 
     def greet(there):
         pl.semaphore_signal(barrier, 1, device_id=there, device_id_type=MESH)
 
     for p in peers:
         greet(group_at(p))
-    for m in mates:
-        greet(plane_at(m))
-    for present, there in (
-        (has_lo, layer_at(layer - 1)), (has_hi, layer_at(layer + 1)),
-        (has_top, strip_at(strip - 1)), (has_bottom, strip_at(strip + 1)),
-    ):
+    for n in range(4):
+        @pl.when(jnp.logical_not(owns & (post == n)))
+        def _(n=n):
+            greet(plane_at(n))
+
+    sides = (
+        (has_hi, 1, 0), (has_lo, -1, 0), (has_bottom, 0, 1), (has_top, 0, -1),
+        (has_hi & has_bottom, 1, 1), (has_hi & has_top, 1, -1),
+        (has_lo & has_bottom, -1, 1), (has_lo & has_top, -1, -1),
+    )
+    for present, up, down in sides:
         @pl.when(present)
-        def _(there=there):
-            greet(there)
+        def _(up=up, down=down):
+            greet(block_at(up, down))
 
     for f0 in range(NF):
         @pl.when(jnp.logical_not(mine & (f == f0)))
@@ -109,8 +123,8 @@
 
     lax.fori_loop(0, NS, stack, 0)
 
-    expected = len(peers) + len(mates) + NF - mine.astype(jnp.int32)
-    for present in (has_lo, has_hi, has_top, has_bottom):
+    expected = len(peers) + 4 + NF - mine.astype(jnp.int32) - owns.astype(jnp.int32)
+    for present, _, _ in sides:
         expected += present.astype(jnp.int32)
     pl.semaphore_wait(barrier, expected)
 
@@ -120,7 +134,7 @@
             dst_ref=pieces_in.at[f],
             send_sem=piece_send.at[group],
             recv_sem=piece_recv.at[f],
-            device_id={"freq": deep, "slab": 4 * group + wide, "xy": b},
+            device_id={"freq": home, "slab": 4 * swung(b, group) + swung(home, post), "xy": b},
             device_id_type=MESH,
         )
 
@@ -133,11 +147,37 @@
     def _():
         pieces_in[f] = pieces_out[deep]
 
+    def spec_copy(o, k):
+        return pltpu.make_async_remote_copy(
+            src_ref=outgoing.at[o, k],
+            dst_ref=fresh.at[f, k],
+            send_sem=spec_send.at[o, k],
+            recv_sem=spec_recv.at[f, k],
+            device_id=group_at(peers[o]),
+            device_id_type=MESH,
+        )
+
+    def send_spectra(k):
+        for o in range(NF - 1):
+            for w in range(2):
+                outgoing[o, k, w] = turned(raw[o, w, k]).astype(BF16)
+            spec_copy(o, k).start()
+        for w in range(2):
+            fresh[f, k, w] = turned(raw[NF - 1, w, k]).astype(BF16)
+
+    for o in range(NF):
+        for w in range(2):
+            raw_copy(o, w).wait()
+
+    for k in range(AHEAD):
+        send_spectra(k)
+
     cell = rec_ref[...]
-    depth, row, col = (cell >> 16) - first_plane, ((cell >> 9) & (NY - 1)) - first_row, cell & (COLS - 1)
-    here = (depth >= 0) & (depth < DEEP) & (row >= 0) & (row < WIDE)
-    row = jnp.where(here, depth * WIDE + row, -1)
-    at_row = lax.broadcasted_iota(jnp.int32, (ROWS, cell.shape[1]), 0) == row
+    depth, row, col = (cell >> 16) - first_plane + 1, ((cell >> 9) & (NY - 1)) - first_row, cell & (COLS - 1)
+    here = (depth >= 0) & (depth < DEEP + 2) & (row >= -1) & (row <= WIDE)
+    row = jnp.where(here, depth * RING + (row & (RING - 1)), -1)
+    size = (DEEP + 2) * RING
+    at_row = lax.broadcasted_iota(jnp.int32, (size, cell.shape[1]), 0) == row
     at_col = (lax.broadcasted_iota(jnp.int32, (COLS, cell.shape[1]), 0) == col).astype(F32).astype(BF16)
 
     def inject(t, carry):
@@ -150,10 +190,9 @@
             jnp.concatenate([first, second, third], axis=0), at_col,
             (((1,), (1,)), ((), ())), preferred_element_type=F32,
         )
-        inj[t] = (parts[:ROWS] + parts[ROWS : 2 * ROWS] + parts[2 * ROWS :]).reshape(DEEP, WIDE, COLS)
-        return carry
-
-    lax.fori_loop(0, STEPS, inject, 0)
+        total = parts[:size] + parts[size : 2 * size] + parts[2 * size :]
+        inj[t] = total.reshape(DEEP + 2, RING, COLS)
+        return carry
 
     terms = NF * TERMS
     step_of = lax.broadcasted_iota(jnp.int32, (STEPS, STEPS * HALF), 1) // HALF
@@ -167,14 +206,18 @@
         mix[pl.ds(pl.multiple_of(k * HALF, HALF), HALF), :] = values.astype(BF16)
         return carry
 
-    lax.fori_loop(0, terms, fill, 0)
-
-    for o in range(NF):
-        for w in range(2):
-            raw_copy(o, w).wait()
-
-    row_id = lax.broadcasted_iota(jnp.int32, (WIDE, COLS), 0)
-    col_id = lax.broadcasted_iota(jnp.int32, (WIDE, COLS), 1)
+    def clear_plane(p, carry):
+        for n in range(2):
+            for w in range(2):
+                field[n, p, w] = jnp.zeros((RING, COLS), F32)
+
+        @pl.when(p < DEEP + 2)
+        def _():
+            cour[p] = jnp.zeros((RING, COLS), F32)
+
+        return carry
+
+    lax.fori_loop(0, DEEP + 4, clear_plane, 0)
 
     for f0 in range(NF):
         @pl.when(jnp.logical_not(mine & (f == f0)))
@@ -188,139 +231,199 @@
         cols = pl.ds(128 * f0, 128)
         for p in range(DEEP):
             for w in range(2):
-                field[1, p, w, :, cols] = pieces_in[f0, w, p]
-                field[0, p, w, :, cols] = pieces_in[f0, 2 + w, p]
-            cour[p, :, cols] = pieces_in[f0, 4, p]
-
-    def z_copy(s, up):
+                field[1, p + 2, w, pl.ds(0, WIDE), cols] = pieces_in[f0, w, p]
+                field[0, p + 2, w, pl.ds(0, WIDE), cols] = pieces_in[f0, 2 + w, p]
+            cour[p + 1, pl.ds(0, WIDE), cols] = pieces_in[f0, 4, p]
+
+    def halo_copy(r, up, down):
+        if not down:
+            low = up > 0
+            src, dst = planes.at[2 * r, pl.ds(DEEP - 2 if low else 0, 2)], (lo if low else hi).at[r]
+            sems = zsend.at[r, int(low)], zrecv.at[r, int(low)]
+        elif not up:
+            n = int(down > 0)
+            src, dst, sems = yout.at[r, n], yin.at[r, n], (ysend.at[r, n], yrecv.at[r, n])
+        else:
+            n, m = int(down > 0), int(up > 0)
+            src, dst = corner_out.at[r, m, n], corner.at[r, m, n]
+            sems = csend.at[r, 2 * m + n], crecv.at[r, 2 * m + n]
         return pltpu.make_async_remote_copy(
-            src_ref=planes.at[s, DEEP - 1 if up else 0],
-            dst_ref=(lo if up else hi).at[s],
-            send_sem=zsend.at[s, int(up)],
-            recv_sem=zrecv.at[s, int(up)],
-            device_id=layer_at(layer + 1 if up else layer - 1),
-            device_id_type=MESH,
+            src_ref=src, dst_ref=dst, send_sem=sems[0], recv_sem=sems[1],
+            device_id=block_at(up, down), device_id_type=MESH,
         )
 
-    def y_copy(s, down):
+    def first_copy(up, down):
+        n = int(up + down > 0)
+        if up:
+            src, dst, m = first_z.at[n], (first_lo if n else first_hi), n
+        else:
+            src, dst, m = first_y.at[n], first_in.at[n], 2 + n
         return pltpu.make_async_remote_copy(
-            src_ref=yout.at[s, int(down)],
-            dst_ref=yin.at[s, int(down)],
-            send_sem=ysend.at[s, int(down)],
-            recv_sem=yrecv.at[s, int(down)],
-            device_id=strip_at(strip + 1 if down else strip - 1),
-            device_id_type=MESH,
+            src_ref=src, dst_ref=dst, send_sem=fsend.at[m], recv_sem=frecv.at[m],
+            device_id=block_at(up, down), device_id_type=MESH,
         )
-
-    directions = (
-        (has_hi, z_copy, True), (has_lo, z_copy, False), (has_bottom, y_copy, True), (has_top, y_copy, False)
-    )
 
     def publish(s, p, values):
         planes[s, p] = jnp.concatenate(values, axis=0).astype(BF16)
-        for w in range(2):
-            yout[s, 0, pl.ds(2 * p + w, 1), :] = values[w][0:1]
-            yout[s, 1, pl.ds(2 * p + w, 1), :] = values[w][WIDE - 1 : WIDE]
-
-    def send(s):
-        for present, copy, forward in directions:
+
+    def send(r, values):
+        for present, up, down in sides[:2]:
             @pl.when(present)
-            def _(copy=copy, forward=forward):
-                copy(s, forward).start()
-
-    def spec_copy(o, k):
-        return pltpu.make_async_remote_copy(
-            src_ref=outgoing.at[o, k],
-            dst_ref=fresh.at[f, k],
-            send_sem=spec_send.at[o, k],
-            recv_sem=spec_recv.at[f, k],
-            device_id=group_at(peers[o]),
-            device_id_type=MESH,
-        )
-
-    def send_spectra(k):
-        for o in range(NF - 1):
-            for w in range(2):
-                outgoing[o, k, w] = turned(raw[o, w, k]).astype(BF16)
-            spec_copy(o, k).start()
-        for w in range(2):
-            fresh[f, k, w] = turned(raw[NF - 1, w, k]).astype(BF16)
+            def _(up=up, down=down):
+                halo_copy(r, up, down).start()
+
+        for n, at in ((0, 0), (1, WIDE - 2)):
+            rows = [values[p][w][at : at + 2] for p in range(DEEP) for w in range(2)]
+            yout[r, n] = jnp.concatenate(rows, axis=0).astype(BF16)
+        for m, p in ((0, 0), (1, DEEP - 1)):
+            for n, at in ((0, 0), (1, WIDE - 1)):
+                rows = [
+                    values[p][w][at : at + 1, 128 * c : 128 * (c + 1)] for w in range(2) for c in range(4)
+                ]
+                corner_out[r, m, n] = jnp.concatenate(rows, axis=0)
+        for present, up, down in sides[2:]:
+            @pl.when(present)
+            def _(up=up, down=down):
+                halo_copy(r, up, down).start()
 
     def held_copy(n, batch):
         return pltpu.make_async_remote_copy(
-            src_ref=planes.at[pl.ds(4 * batch + 1, 4), mates[n]],
+            src_ref=planes.at[pl.ds(4 * batch + 1, 4), n],
             dst_ref=held.at[pl.ds(4 * batch, 4), wide],
             send_sem=held_send.at[batch, n],
             recv_sem=held_recv.at[batch, wide],
-            device_id=plane_at(mates[n]),
+            device_id=plane_at(n),
             device_id_type=MESH,
         )
 
+    initial = [[field[0, p + 2, w, pl.ds(0, WIDE), :] for w in range(2)] for p in range(DEEP)]
     for p in range(DEEP):
-        publish(0, p, [field[0, p, w] for w in range(2)])
-    send(0)
-
+        publish(0, p, initial[p])
+    send(0, initial)
+
+    for n, p, row in ((0, 0, 0), (1, DEEP - 1, WIDE - 1)):
+        for w in range(2):
+            first_z[n, w] = field[1, p + 2, w, pl.ds(0, WIDE), :]
+            for q in range(DEEP):
+                first_y[n, pl.ds(DEEP * w + q, 1), :] = field[1, q + 2, w, pl.ds(row, 1), :]
+        first_z[n, 2] = cour[p + 1, pl.ds(0, WIDE), :]
+        for q in range(DEEP):
+            first_y[n, pl.ds(2 * DEEP + q, 1), :] = cour[q + 1, pl.ds(row, 1), :]
+        first_y[n, pl.ds(3 * DEEP, DEEP), :] = jnp.zeros((DEEP, COLS), F32)
+    for present, up, down in sides[:4]:
+        @pl.when(present)
+        def _(up=up, down=down):
+            first_copy(up, down).start()
+
+    for present, up, down in sides[:4]:
+        @pl.when(present)
+        def _(up=up, down=down):
+            first_copy(-up, -down).wait_recv()
+            if up:
+                there, at = (first_hi, DEEP + 2) if up > 0 else (first_lo, 1)
+                for w in range(2):
+                    field[1, at, w, pl.ds(0, WIDE), :] = there[w]
+                cour[at - 1, pl.ds(0, WIDE), :] = there[2]
+            else:
+                n, at = (0, WIDE) if down > 0 else (1, RING - 1)
+                for q in range(DEEP):
+                    for w in range(2):
+                        field[1, q + 2, w, pl.ds(at, 1), :] = first_in[n, pl.ds(DEEP * w + q, 1), :]
+                    cour[q + 1, pl.ds(at, 1), :] = first_in[n, pl.ds(2 * DEEP + q, 1), :]
+
+    row_id = lax.broadcasted_iota(jnp.int32, (RING, COLS), 0)
+    col_id = lax.broadcasted_iota(jnp.int32, (RING, COLS), 1)
     source = src_ref[0]
     source_row = ((source >> 9) & (NY - 1)) - first_row
-    source_plane = (source >> 16) - first_plane
+    source_row = jnp.where((source_row >= -1) & (source_row <= WIDE), source_row & (RING - 1), -1)
+    source_plane = (source >> 16) - first_plane + 2
     at_source = (row_id == source_row) & (col_id == (source & (COLS - 1)))
 
-    def arrivals(s, present, copy, there):
-        @pl.when(present)
+    def step(t, now, p, w, height):
+        u = field[now, p, w]
+        beside = pltpu.roll(u, 1, 0)[:height] + pltpu.roll(u, RING - 1, 0)[:height]
+        u = u[:height]
+        beside += field[now, p - 1, w, pl.ds(0, height), :] + field[now, p + 1, w, pl.ds(0, height), :]
+        col = col_id[:height]
+        beside += jnp.where(col == 0, 0.0, pltpu.roll(u, 1, 1))
+        beside += jnp.where(col == COLS - 1, 0.0, pltpu.roll(u, COLS - 1, 1))
+        if w == 1:
+            injection = inj[t, p - 1, pl.ds(0, height), :]
+        else:
+            injection = jnp.where(at_source[:height] & (source_plane == p), wav_ref[t], 0.0)
+        before = field[1 - now, p, w, pl.ds(0, height), :]
+        following = 2.0 * u - before + cour[p - 1, pl.ds(0, height), :] * (beside - 6.0 * u) + injection
+        field[1 - now, p, w, pl.ds(0, height), :] = following
+        return following
+
+    def advance(r, carry):
+        for i in range(EACH):
+            k = AHEAD + EACH * r + i
+
+            @pl.when(k < BESIDE)
+            def _(k=k):
+                send_spectra(k)
+
+        lax.fori_loop(2 * r, 2 * r + 2, inject, 0)
+        share = terms // ROUNDS
+        lax.fori_loop(share * r, share * (r + 1), fill, 0)
+
+        for present, up, down in sides:
+            @pl.when(present)
+            def _(up=up, down=down):
+                halo_copy(r, -up, -down).wait_recv()
+                if not down:
+                    there, at = (hi, DEEP + 2) if up > 0 else (lo, 0)
+                    for q in range(2):
+                        both = there[r, q].astype(F32)
+                        for w in range(2):
+                            field[0, at + q, w, pl.ds(0, WIDE), :] = both[WIDE * w : WIDE * (w + 1)]
+                    return
+                n, at = (0, WIDE) if down > 0 else (1, RING - 2)
+                if not up:
+                    rows = yin[r, n].astype(F32)
+                    for p in range(DEEP):
+                        for w in range(2):
+                            i = 4 * p + 2 * w
+                            field[0, p + 2, w, pl.ds(at, 2), :] = rows[i : i + 2]
+                else:
+                    m, q = (0, DEEP + 2) if up > 0 else (1, 1)
+                    at = WIDE if down > 0 else RING - 1
+                    for w in range(2):
+                        for c in range(4):
+                            field[0, q, w, pl.ds(at, 1), pl.ds(128 * c, 128)] = corner[
+                                r, m, n, pl.ds(4 * w + c, 1), :
+                            ]
+
+        t = 2 * r
+        middle = [
+            [step(t, 0, p, w, RING if 1 < p < DEEP + 2 else WIDE) for w in range(2)]
+            for p in range(1, DEEP + 3)
+        ]
+        last = [[step(t + 1, 1, p, w, WIDE) for w in range(2)] for p in range(2, DEEP + 2)]
+        for p in range(DEEP):
+            publish(t + 2, p, last[p])
+
+        @pl.when(r < ROUNDS - 1)
         def _():
-            copy.wait_recv()
-
-        @pl.when(jnp.logical_not(present))
+            send(r + 1, last)
+
+        for p in range(DEEP):
+            publish(t + 1, p, [values[:WIDE] for values in middle[p + 1]])
+
+        @pl.when(owns)
         def _():
-            there[s] = jnp.zeros(there.shape[1:], there.dtype)
-
-    def advance(t, carry):
-        now, other = t % 2, (t + 1) % 2
-
-        @pl.when(t < BESIDE)
-        def _():
-            send_spectra(t)
-
-        arrivals(t, has_lo, z_copy(t, True), lo)
-        arrivals(t, has_hi, z_copy(t, False), hi)
-        arrivals(t, has_top, y_copy(t, True), yin.at[:, 1])
-        arrivals(t, has_bottom, y_copy(t, False), yin.at[:, 0])
-        below = [lo[t].astype(F32)[WIDE * w : WIDE * (w + 1)] for w in range(2)]
-        above = [hi[t].astype(F32)[WIDE * w : WIDE * (w + 1)] for w in range(2)]
-        for p in range(DEEP):
-            values = []
-            for w in range(2):
-                u = field[now, p, w]
-                beside = (field[now, p - 1, w] if p else below[w])
-                beside += (field[now, p + 1, w] if p < DEEP - 1 else above[w])
-                top, bottom = (yin[t, d, pl.ds(2 * p + w, 1), :] for d in (1, 0))
-                beside += jnp.where(row_id == 0, top, pltpu.roll(u, 1, 0))
-                beside += jnp.where(row_id == WIDE - 1, bottom, pltpu.roll(u, WIDE - 1, 0))
-                beside += jnp.where(col_id == 0, 0.0, pltpu.roll(u, 1, 1))
-                beside += jnp.where(col_id == COLS - 1, 0.0, pltpu.roll(u, COLS - 1, 1))
-                if w == 1:
-                    injection = inj[t, p]
-                else:
-                    injection = jnp.where(at_source & (source_plane == p), wav_ref[t], 0.0)
-                following = 2.0 * u - field[other, p, w] + cour[p] * (beside - 6.0 * u) + injection
-                field[other, p, w] = following
-                values.append(following)
-            publish(t + 1, p, values)
-
-        @pl.when(t < STEPS - 1)
-        def _():
-            send(t + 1)
-
-        held[t, wide] = planes[t + 1, wide]
-
-        @pl.when(t % 4 == 3)
-        def _():
-            for n in range(3):
-                held_copy(n, t // 4).start()
-
-        return carry
-
-    lax.fori_loop(0, STEPS, advance, 0)
+            for i in (1, 2):
+                held[t + i - 1, wide] = planes[t + i, post]
+
+        for n in range(4):
+            @pl.when((r % 2 == 1) & jnp.logical_not(owns & (post == n)))
+            def _(n=n):
+                held_copy(n, r // 2).start()
+
+        return carry
+
+    lax.fori_loop(0, ROUNDS, advance, 0)
 
     def rest(k, carry):
         send_spectra(k)
@@ -329,13 +432,15 @@
     lax.fori_loop(BESIDE, TERMS, rest, 0)
 
     def turn_batch(batch, carry):
-        for n in range(3):
-            pltpu.make_async_remote_copy(
-                src_ref=planes.at[pl.ds(4 * batch + 1, 4), mates[n]],
-                dst_ref=held.at[pl.ds(4 * batch, 4), mates[n]],
-                send_sem=held_send.at[batch, n], recv_sem=held_recv.at[batch, mates[n]],
-                device_id=plane_at(mates[n]), device_id_type=MESH,
-            ).wait_recv()
+        for n in range(4):
+            @pl.when(jnp.logical_not(owns & (post == n)))
+            def _(n=n):
+                pltpu.make_async_remote_copy(
+                    src_ref=planes.at[pl.ds(4 * batch + 1, 4), n],
+                    dst_ref=held.at[pl.ds(4 * batch, 4), swung(f, n)],
+                    send_sem=held_send.at[batch, n], recv_sem=held_recv.at[batch, swung(f, n)],
+                    device_id=plane_at(n), device_id_type=MESH,
+                ).wait_recv()
 
         def turn(q, inner):
             t = 4 * batch + q
@@ -440,21 +545,34 @@
 
     lax.fori_loop(0, lags, finish, 0)
 
-    def sent(s, carry):
-        for present, copy, forward in directions:
+    def sent(r, carry):
+        for present, up, down in sides:
             @pl.when(present)
-            def _(copy=copy, forward=forward):
-                copy(s, forward).wait_send()
-
+            def _(up=up, down=down):
+                halo_copy(r, up, down).wait_send()
+
+        return carry
+
+    lax.fori_loop(0, ROUNDS, sent, 0)
+
+    for present, up, down in sides[:4]:
+        @pl.when(present)
+        def _(up=up, down=down):
+            first_copy(up, down).wait_send()
+
+    def spectra_sent(k, carry):
         for o in range(NF - 1):
-            spec_copy(o, s).wait_send()
-        return carry
-
-    lax.fori_loop(0, STEPS, sent, 0)
+            spec_copy(o, k).wait_send()
+        return carry
+
+    lax.fori_loop(0, TERMS, spectra_sent, 0)
 
     def delivered(batch, carry):
-        for n in range(3):
-            held_copy(n, batch).wait_send()
+        for n in range(4):
+            @pl.when(jnp.logical_not(owns & (post == n)))
+            def _(n=n):
+                held_copy(n, batch).wait_send()
+
         return carry
 
     lax.fori_loop(0, STEPS // 4, delivered, 0)
@@ -486,15 +604,22 @@
             pltpu.VMEM((NF, TERMS, 2, XS, XS), BF16),
             pltpu.VMEM((4, 5, DEEP, WIDE, 128), F32),
             pltpu.VMEM((NF, 5, DEEP, WIDE, 128), F32),
-            pltpu.VMEM((2, DEEP, 2, WIDE, COLS), F32),
-            pltpu.VMEM((DEEP, WIDE, COLS), F32),
-            pltpu.VMEM((STEPS, DEEP, WIDE, COLS), F32),
+            pltpu.VMEM((2, DEEP + 4, 2, RING, COLS), F32),
+            pltpu.VMEM((DEEP + 2, RING, COLS), F32),
+            pltpu.VMEM((STEPS, DEEP + 2, RING, COLS), F32),
             pltpu.VMEM((STEPS + 1, DEEP) + pair, BF16),
             pltpu.VMEM((STEPS, 4) + pair, BF16),
-            pltpu.VMEM((STEPS,) + pair, BF16),
-            pltpu.VMEM((STEPS,) + pair, BF16),
-            pltpu.VMEM((STEPS + 1, 2, 2 * DEEP, COLS), F32),
-            pltpu.VMEM((STEPS, 2, 2 * DEEP, COLS), F32),
+            pltpu.VMEM((ROUNDS, 2) + pair, BF16),
+            pltpu.VMEM((ROUNDS, 2) + pair, BF16),
+            pltpu.VMEM((ROUNDS, 2, 4 * DEEP, COLS), BF16),
+            pltpu.VMEM((ROUNDS, 2, 4 * DEEP, COLS), BF16),
+            pltpu.VMEM((ROUNDS, 2, 2, 8, 128), F32),
+            pltpu.VMEM((ROUNDS, 2, 2, 8, 128), F32),
+            pltpu.VMEM((2, 3, WIDE, COLS), F32),
+            pltpu.VMEM((2, 4 * DEEP, COLS), F32),
+            pltpu.VMEM((3, WIDE, COLS), F32),
+            pltpu.VMEM((3, WIDE, COLS), F32),
+            pltpu.VMEM((2, 4 * DEEP, COLS), F32),
             pltpu.VMEM((terms, STEPS * HALF), F32),
             pltpu.VMEM((terms * HALF, STEPS * HALF), BF16),
             pltpu.VMEM((2, XS // HALF // 2, STEPS, HALF, 2 * XS), BF16),
@@ -506,11 +631,15 @@
             dma((NF, TERMS)),
             dma((4,)),
             dma((NF,)),
-            dma((STEPS, 2)),
-            dma((STEPS, 2)),
-            dma((STEPS, 2)),
-            dma((STEPS, 2)),
-            dma((STEPS // 4, 3)),
+            dma((ROUNDS, 2)),
+            dma((ROUNDS, 2)),
+            dma((ROUNDS, 2)),
+            dma((ROUNDS, 2)),
+            dma((ROUNDS, 4)),
+            dma((ROUNDS, 4)),
+            dma((4,)),
+            dma((4,)),
+            dma((STEPS // 4, 4)),
             dma((STEPS // 4, 4)),
         ],
         compiler_params=pltpu.CompilerParams(

time: 162 us -> 141 us (0.87)
  the two profiles are of different devices: /device:TPU:25 before, /device:TPU:1 now
where the time goes in v3:
time: 141 us
  Pallas kernels  137 us (97%)
  local copies, waits for them, and re-layouts  2.61 us (2%)
    pallas_call x1, Pallas kernels, body(): pl.pallas_call(kernel, out_shape=jax.ShapeDtypeStruct((lags, ROWS, COLS),...  137 us

profile of v3, /device:TPU:1, one launch (start us, length us, event | category | flops | bytes accessed | tf_op | source)
XLA Modules:
  0.0 141.2 jit_solution(7900476487589176868)
XLA Ops:
  0.7 0.8 cosine_convert_fusion
  1.5 0.1 copy.14
  1.6 0.6 copy.15
  2.2 137.1 %window_image.1 = bf16[17,32,512]{2,1,0:T(8,128)(2,1)} custom-call(f32[2,16,8,128]{3,2,1,0:T(8,128)} %prev_ref.1, f32[2,16,8,128]{3,2,1,0:T(8,128)} %cur_ref.1, f32[16,8,128]{2,1,0:T(8,128)} %cour_ref.1, f32[16]{0:T(128)} %wav_ref.1, f32[16,256]{1,0:T(8,128)} %traces_ref.1, s32[1]{0:T(128)S(6)} %copy.18.src_ref, s32[1,256]{1,0:T(1,128)} %bitcast.13, ...), custom_call_target="tpu_custom_call" | custom-call | tf_op jit(solution)/shard_map/window_image/pallas_call | solution.py:596
  139.3 1.9 %copy.19 = bf16[17,1,1,32,512]{4,3,2,1,0:T(8,128)(2,1)} copy(bf16[17,1,1,32,512]{4,3,2,1,0:T(8,128)(2,1)} %bitcast.10) | data formatting | bytes 1114112
  (2 shorter events, 0.0 us)

commit v4 on v3

--- a/solution.py
+++ b/solution.py
@@ -22,7 +22,7 @@
 HALF = 16
 ROUND = 2
 ROUNDS = STEPS // 2
-AHEAD, EACH, BESIDE = 2, 1, 10
+AHEAD, EACH, BESIDE = 1, 1, 9
 MESH = pl.DeviceIdType.MESH
 
 
@@ -44,9 +44,9 @@
 def kernel(
     prev_ref, cur_ref, cour_ref, wav_ref, traces_ref, src_ref, rec_ref, lag_ref, table_ref, spec_ref,
     out,
-    raw, outgoing, fresh, pieces_out, pieces_in, field, cour, inj, planes, held, lo, hi, yout, yin, corner_out, corner, first_z, first_y, first_lo, first_hi, first_in,
+    raw, outgoing, fresh, pieces_out, relay, pieces_in, field, cour, inj, planes, held, lo, hi, yout, yin, corner_out, corner, first_z, first_y, first_lo, first_hi, first_in,
     spread, mix, snaps, early, late, sums,
-    raw_sem, spec_send, spec_recv, piece_send, piece_recv,
+    raw_sem, spec_send, spec_recv, relay_send, relay_recv, piece_send, piece_recv,
     zsend, zrecv, ysend, yrecv, csend, crecv, fsend, frecv, held_send, held_recv,
 ):
     f, j, b = lax.axis_index("freq"), lax.axis_index("slab"), lax.axis_index("xy")
@@ -86,7 +86,7 @@
             raw_copy(o, w).start()
 
     barrier = pltpu.get_barrier_semaphore()
-    mine = (home == f) & (f % 2 == 0)
+    mine = f % 2 == 0
 
     def greet(there):
         pl.semaphore_signal(barrier, 1, device_id=there, device_id_type=MESH)
@@ -108,44 +108,75 @@
         def _(up=up, down=down):
             greet(block_at(up, down))
 
+    for n in range(4):
+        @pl.when(home != n)
+        def _(n=n):
+            greet({"freq": f, "slab": 4 * n + post, "xy": b})
+
     for f0 in range(NF):
         @pl.when(jnp.logical_not(mine & (f == f0)))
         def _(f0=f0):
-            greet({"freq": f0, "slab": 4 * f + wide, "xy": b})
-
-    def stack(i, carry):
-        group, p = i // DEEP, i % DEEP
+            greet({"freq": f0, "slab": 4 * home + wide, "xy": b})
+
+    def stack(group, carry):
+        at = pl.ds(group * DEEP, DEEP)
         for w in range(2):
-            pieces_out[group, w, p] = prev_ref[w, i]
-            pieces_out[group, 2 + w, p] = cur_ref[w, i]
-        pieces_out[group, 4, p] = cour_ref[i]
-        return carry
-
-    lax.fori_loop(0, NS, stack, 0)
-
-    expected = len(peers) + 4 + NF - mine.astype(jnp.int32) - owns.astype(jnp.int32)
+            pieces_out[group, w] = prev_ref[w, at].reshape(DEEP * WIDE, 128).astype(BF16)
+            pieces_out[group, 2 + w] = cur_ref[w, at].reshape(DEEP * WIDE, 128).astype(BF16)
+        pieces_out[group, 4] = cour_ref[at].reshape(DEEP * WIDE, 128).astype(BF16)
+        return carry
+
+    lax.fori_loop(0, 4, stack, 0)
+
+    expected = len(peers) + 4 + 3 + NF - mine.astype(jnp.int32) - owns.astype(jnp.int32)
     for present, _, _ in sides:
         expected += present.astype(jnp.int32)
     pl.semaphore_wait(barrier, expected)
 
-    def piece_copy(group):
+    def relay_copy(n):
+        group = swung(b, n)
         return pltpu.make_async_remote_copy(
             src_ref=pieces_out.at[group],
-            dst_ref=pieces_in.at[f],
-            send_sem=piece_send.at[group],
-            recv_sem=piece_recv.at[f],
-            device_id={"freq": home, "slab": 4 * swung(b, group) + swung(home, post), "xy": b},
+            dst_ref=relay.at[home],
+            send_sem=relay_send.at[n],
+            recv_sem=relay_recv.at[home],
+            device_id={"freq": f, "slab": 4 * n + post, "xy": b},
             device_id_type=MESH,
         )
 
-    for group in range(4):
-        @pl.when(jnp.logical_not(mine & (deep == group)))
-        def _(group=group):
-            piece_copy(group).start()
+    def piece_copy(n):
+        return pltpu.make_async_remote_copy(
+            src_ref=relay.at[n],
+            dst_ref=pieces_in.at[f],
+            send_sem=piece_send.at[n],
+            recv_sem=piece_recv.at[f],
+            device_id={"freq": n, "slab": 4 * home + swung(n, post), "xy": b},
+            device_id_type=MESH,
+        )
+
+    for n in range(4):
+        @pl.when(home != n)
+        def _(n=n):
+            relay_copy(n).start()
+
+    relay[home] = pieces_out[deep]
+
+    for n in range(4):
+        @pl.when(home != n)
+        def _(n=n):
+            pltpu.make_async_remote_copy(
+                src_ref=pieces_out.at[n], dst_ref=relay.at[n],
+                send_sem=relay_send.at[n], recv_sem=relay_recv.at[n],
+                device_id={"freq": f, "slab": 4 * n + post, "xy": b}, device_id_type=MESH,
+            ).wait_recv()
+
+        @pl.when(jnp.logical_not(mine & (f == n)))
+        def _(n=n):
+            piece_copy(n).start()
 
     @pl.when(mine)
     def _():
-        pieces_in[f] = pieces_out[deep]
+        pieces_in[f] = relay[f]
 
     def spec_copy(o, k):
         return pltpu.make_async_remote_copy(
@@ -229,11 +260,13 @@
             ).wait_recv()
 
         cols = pl.ds(128 * f0, 128)
+        piece = [pieces_in[f0, n].astype(F32) for n in range(5)]
         for p in range(DEEP):
+            rows = slice(WIDE * p, WIDE * (p + 1))
             for w in range(2):
-                field[1, p + 2, w, pl.ds(0, WIDE), cols] = pieces_in[f0, w, p]
-                field[0, p + 2, w, pl.ds(0, WIDE), cols] = pieces_in[f0, 2 + w, p]
-            cour[p + 1, pl.ds(0, WIDE), cols] = pieces_in[f0, 4, p]
+                field[1, p + 2, w, pl.ds(0, WIDE), cols] = piece[w][rows]
+                field[0, p + 2, w, pl.ds(0, WIDE), cols] = piece[2 + w][rows]
+            cour[p + 1, pl.ds(0, WIDE), cols] = piece[4][rows]
 
     def halo_copy(r, up, down):
         if not down:
@@ -577,10 +610,14 @@
 
     lax.fori_loop(0, STEPS // 4, delivered, 0)
 
-    for group in range(4):
-        @pl.when(jnp.logical_not(mine & (deep == group)))
-        def _(group=group):
-            piece_copy(group).wait_send()
+    for n in range(4):
+        @pl.when(home != n)
+        def _(n=n):
+            relay_copy(n).wait_send()
+
+        @pl.when(jnp.logical_not(mine & (f == n)))
+        def _(n=n):
+            piece_copy(n).wait_send()
 
 
 def body(
@@ -602,8 +639,9 @@
             pltpu.VMEM((NF, 2, TERMS, ROWS, COLS), F32),
             pltpu.VMEM((NF - 1, TERMS, 2, XS, XS), BF16),
             pltpu.VMEM((NF, TERMS, 2, XS, XS), BF16),
-            pltpu.VMEM((4, 5, DEEP, WIDE, 128), F32),
-            pltpu.VMEM((NF, 5, DEEP, WIDE, 128), F32),
+            pltpu.VMEM((4, 5, DEEP * WIDE, 128), BF16),
+            pltpu.VMEM((4, 5, DEEP * WIDE, 128), BF16),
+            pltpu.VMEM((NF, 5, DEEP * WIDE, 128), BF16),
             pltpu.VMEM((2, DEEP + 4, 2, RING, COLS), F32),
             pltpu.VMEM((DEEP + 2, RING, COLS), F32),
             pltpu.VMEM((STEPS, DEEP + 2, RING, COLS), F32),
@@ -630,6 +668,8 @@
             dma((NF - 1, TERMS)),
             dma((NF, TERMS)),
             dma((4,)),
+            dma((4,)),
+            dma((4,)),
             dma((NF,)),
             dma((ROUNDS, 2)),
             dma((ROUNDS, 2)),

time: 141 us -> 135 us (0.957)
  Pallas kernels: 137 us -> 131 us
    pallas_call x1, Pallas kernels: 137 us -> 131 us  [body(): pl.pallas_call(kernel, out_shape=jax.ShapeDtypeStruct((lags, ROWS, COLS),...]
where the time goes in v4:
time: 135 us
  Pallas kernels  131 us (97%)
  local copies, waits for them, and re-layouts  2.61 us (2%)
    pallas_call x1, Pallas kernels, body(): pl.pallas_call(kernel, out_shape=jax.ShapeDtypeStruct((lags, ROWS, COLS),...  131 us

profile of v4, /device:TPU:1, one launch (start us, length us, event | category | flops | bytes accessed | tf_op | source)
XLA Modules:
  0.0 135.1 jit_solution(4004059811614713594)
XLA Ops:
  0.7 0.8 cosine_convert_fusion
  1.5 0.1 copy.14
  1.6 0.6 copy.15
  2.2 131.0 %window_image.1 = bf16[17,32,512]{2,1,0:T(8,128)(2,1)} custom-call(f32[2,16,8,128]{3,2,1,0:T(8,128)} %prev_ref.1, f32[2,16,8,128]{3,2,1,0:T(8,128)} %cur_ref.1, f32[16,8,128]{2,1,0:T(8,128)} %cour_ref.1, f32[16]{0:T(128)} %wav_ref.1, f32[16,256]{1,0:T(8,128)} %traces_ref.1, s32[1]{0:T(128)S(6)} %copy.18.src_ref, s32[1,256]{1,0:T(1,128)} %bitcast.13, ...), custom_call_target="tpu_custom_call" | custom-call | tf_op jit(solution)/shard_map/window_image/pallas_call | solution.py:633
  133.2 1.9 %copy.19 = bf16[17,1,1,32,512]{4,3,2,1,0:T(8,128)(2,1)} copy(bf16[17,1,1,32,512]{4,3,2,1,0:T(8,128)(2,1)} %bitcast.10) | data formatting | bytes 1114112
  (2 shorter events, 0.0 us)

commit v5 on v4

--- a/solution.py
+++ b/solution.py
@@ -123,7 +123,10 @@
         for w in range(2):
             pieces_out[group, w] = prev_ref[w, at].reshape(DEEP * WIDE, 128).astype(BF16)
             pieces_out[group, 2 + w] = cur_ref[w, at].reshape(DEEP * WIDE, 128).astype(BF16)
-        pieces_out[group, 4] = cour_ref[at].reshape(DEEP * WIDE, 128).astype(BF16)
+        exact = cour_ref[at].reshape(DEEP * WIDE, 128)
+        rounded = exact.astype(BF16)
+        pieces_out[group, 4] = rounded
+        pieces_out[group, 5] = (exact - rounded.astype(F32)).astype(BF16)
         return carry
 
     lax.fori_loop(0, 4, stack, 0)
@@ -260,13 +263,13 @@
             ).wait_recv()
 
         cols = pl.ds(128 * f0, 128)
-        piece = [pieces_in[f0, n].astype(F32) for n in range(5)]
+        piece = [pieces_in[f0, n].astype(F32) for n in range(6)]
         for p in range(DEEP):
             rows = slice(WIDE * p, WIDE * (p + 1))
             for w in range(2):
                 field[1, p + 2, w, pl.ds(0, WIDE), cols] = piece[w][rows]
                 field[0, p + 2, w, pl.ds(0, WIDE), cols] = piece[2 + w][rows]
-            cour[p + 1, pl.ds(0, WIDE), cols] = piece[4][rows]
+            cour[p + 1, pl.ds(0, WIDE), cols] = piece[4][rows] + piece[5][rows]
 
     def halo_copy(r, up, down):
         if not down:
@@ -639,9 +642,9 @@
             pltpu.VMEM((NF, 2, TERMS, ROWS, COLS), F32),
             pltpu.VMEM((NF - 1, TERMS, 2, XS, XS), BF16),
             pltpu.VMEM((NF, TERMS, 2, XS, XS), BF16),
-            pltpu.VMEM((4, 5, DEEP * WIDE, 128), BF16),
-            pltpu.VMEM((4, 5, DEEP * WIDE, 128), BF16),
-            pltpu.VMEM((NF, 5, DEEP * WIDE, 128), BF16),
+            pltpu.VMEM((4, 6, DEEP * WIDE, 128), BF16),
+            pltpu.VMEM((4, 6, DEEP * WIDE, 128), BF16),
+            pltpu.VMEM((NF, 6, DEEP * WIDE, 128), BF16),
             pltpu.VMEM((2, DEEP + 4, 2, RING, COLS), F32),
             pltpu.VMEM((DEEP + 2, RING, COLS), F32),
             pltpu.VMEM((STEPS, DEEP + 2, RING, COLS), F32),

time: 135 us -> 136 us (level)
  no operation moved by 1% of the time
where the time goes in v5:
time: 136 us
  Pallas kernels  132 us (97%)
  local copies, waits for them, and re-layouts  2.61 us (2%)
    pallas_call x1, Pallas kernels, body(): pl.pallas_call(kernel, out_shape=jax.ShapeDtypeStruct((lags, ROWS, COLS),...  132 us

profile of v5, /device:TPU:1, one launch (start us, length us, event | category | flops | bytes accessed | tf_op | source)
XLA Modules:
  0.0 136.2 jit_solution(1196706158167815504)
XLA Ops:
  0.7 0.8 cosine_convert_fusion
  1.5 0.1 copy.14
  1.6 0.6 copy.15
  2.2 132.1 %window_image.1 = bf16[17,32,512]{2,1,0:T(8,128)(2,1)} custom-call(f32[2,16,8,128]{3,2,1,0:T(8,128)} %prev_ref.1, f32[2,16,8,128]{3,2,1,0:T(8,128)} %cur_ref.1, f32[16,8,128]{2,1,0:T(8,128)} %cour_ref.1, f32[16]{0:T(128)} %wav_ref.1, f32[16,256]{1,0:T(8,128)} %traces_ref.1, s32[1]{0:T(128)S(6)} %copy.18.src_ref, s32[1,256]{1,0:T(1,128)} %bitcast.13, ...), custom_call_target="tpu_custom_call" | custom-call | tf_op jit(solution)/shard_map/window_image/pallas_call | solution.py:636
  134.3 1.9 %copy.19 = bf16[17,1,1,32,512]{4,3,2,1,0:T(8,128)(2,1)} copy(bf16[17,1,1,32,512]{4,3,2,1,0:T(8,128)(2,1)} %bitcast.10) | data formatting | bytes 1114112
  (2 shorter events, 0.0 us)

commit v6 on v5

--- a/solution.py
+++ b/solution.py
@@ -303,11 +303,6 @@
         planes[s, p] = jnp.concatenate(values, axis=0).astype(BF16)
 
     def send(r, values):
-        for present, up, down in sides[:2]:
-            @pl.when(present)
-            def _(up=up, down=down):
-                halo_copy(r, up, down).start()
-
         for n, at in ((0, 0), (1, WIDE - 2)):
             rows = [values[p][w][at : at + 2] for p in range(DEEP) for w in range(2)]
             yout[r, n] = jnp.concatenate(rows, axis=0).astype(BF16)
@@ -317,7 +312,7 @@
                     values[p][w][at : at + 1, 128 * c : 128 * (c + 1)] for w in range(2) for c in range(4)
                 ]
                 corner_out[r, m, n] = jnp.concatenate(rows, axis=0)
-        for present, up, down in sides[2:]:
+        for present, up, down in sides[2:] + sides[:2]:
             @pl.when(present)
             def _(up=up, down=down):
                 halo_copy(r, up, down).start()

time: 136 us -> 136 us (level)
  no operation moved by 1% of the time
where the time goes in v6:
time: 136 us
  Pallas kernels  132 us (97%)
  local copies, waits for them, and re-layouts  2.61 us (2%)
    pallas_call x1, Pallas kernels, body(): pl.pallas_call(kernel, out_shape=jax.ShapeDtypeStruct((lags, ROWS, COLS),...  132 us

profile of v6, /device:TPU:1, one launch (start us, length us, event | category | flops | bytes accessed | tf_op | source)
XLA Modules:
  0.0 136.3 jit_solution(15919276589364429951)
XLA Ops:
  0.7 0.8 cosine_convert_fusion
  1.5 0.1 copy.14
  1.6 0.6 copy.15
  2.2 132.2 %window_image.1 = bf16[17,32,512]{2,1,0:T(8,128)(2,1)} custom-call(f32[2,16,8,128]{3,2,1,0:T(8,128)} %prev_ref.1, f32[2,16,8,128]{3,2,1,0:T(8,128)} %cur_ref.1, f32[16,8,128]{2,1,0:T(8,128)} %cour_ref.1, f32[16]{0:T(128)} %wav_ref.1, f32[16,256]{1,0:T(8,128)} %traces_ref.1, s32[1]{0:T(128)S(6)} %copy.18.src_ref, s32[1,256]{1,0:T(1,128)} %bitcast.13, ...), custom_call_target="tpu_custom_call" | custom-call | tf_op jit(solution)/shard_map/window_image/pallas_call | solution.py:631
  134.4 1.9 %copy.19 = bf16[17,1,1,32,512]{4,3,2,1,0:T(8,128)(2,1)} copy(bf16[17,1,1,32,512]{4,3,2,1,0:T(8,128)(2,1)} %bitcast.10) | data formatting | bytes 1114112
  (2 shorter events, 0.0 us)
